TPU v7x, 512 devices: a whole 4x4x16 slice. The times are simulated.
512 devices in a mesh: dp: 16 (over x, z_lo), work: 32 (over y, z_hi, core).
Axes of the slice: x: 4, y: 4, z: 16 (z_hi: 4, z_lo: 4; z = z_hi * 4 + z_lo), core: 2. Of those that a mesh axis runs over, the one named last changes fastest.
Arguments:
- activations: bfloat16 [16384, 4096], P('dp', 'work'), may hold values from -6 to 6
- gradients: bfloat16 [16384, 8192], P('dp', 'work'), may hold values from -0.125 to 0.125
- left_panels: bfloat16 [32, 1024, 128], P('work'), may hold values from -1 to 2
- panel_slot: int32 [32], replicated, may hold values from 0 to 31, as said below
- right_inverse: bfloat16 [1024, 8192], P(None, 'work'), may hold values from -1 to 2
Outputs:
- input_factor: float32 [1024, 4096], P(None, 'work')
- output_factor: float32 [1024, 8192], P(None, 'work')
- step_update: bfloat16 [4096, 8192], P('dp', 'work')
Inputs may be any that keep to these rules, and one draw needn't show every extreme that they name: `panel_slot`: each slot number appears once.
All inputs are finite; a program needn't handle non-finite values.
Results may differ from a plain program's by a relative error of at most 0.018.
Values may be sent and summed in bfloat16 or wider, within the bound.
No kernel may reach another device: no remote copies, remote signals or barrier semaphores. Data moves between devices by JAX's collectives and lax.ppermute only.
A program may use at most 64 MiB of HBM per device.

v0:
```python
import jax
import jax.numpy as jnp
from jax import lax
from jax.sharding import PartitionSpec as P


def swapped(value, axis, stride):
    mask = 2**stride
    pairs = [(source, source ^ mask) for source in range(lax.axis_size(axis))]
    return lax.ppermute(value, axis, pairs)


def spread(value, axis, source):
    kept = jnp.where(lax.axis_index(axis) == source, value, 0).astype(value.dtype)
    return lax.psum(kept, axis)


def double_up(pieces, position, levels, swapper, concat_dim):
    for degree in range(levels):
        partner = swapper(pieces, degree)
        upper_half = position // (1 << degree) % 2 == 1
        pieces = jnp.where(
            upper_half,
            jnp.concatenate([partner, pieces], concat_dim),
            jnp.concatenate([pieces, partner], concat_dim),
        )
    return pieces


def levels_of(members):
    return members.bit_length() - 1


def contract_rows(first_operand, second_operand):
    return lax.dot_general(
        first_operand, second_operand, (((0,), (0,)), ((), ())), preferred_element_type=jnp.float32
    )


def split_pair(values):
    upper = values.astype(jnp.bfloat16)
    lower = (values - upper.astype(jnp.float32)).astype(jnp.bfloat16)
    return (upper, lower)


def local(activations, gradients, left_panels, panel_slot, right_inverse):
    own_width = activations.shape[1]
    hidden_own = gradients.shape[1]
    block_size = right_inverse.shape[0]
    work_count = lax.axis_size("work")
    data_count = lax.axis_size("dp")
    work_position = lax.axis_index("work")
    data_position = lax.axis_index("dp")
    model_width = own_width * work_count
    total_tokens = activations.shape[0] * data_count
    row_share = model_width // data_count
    whole_x = lax.all_gather(activations, "work", axis=1, tiled=True)
    block_start = work_position * own_width // block_size * block_size
    feature_block = lax.dynamic_slice_in_dim(whole_x, block_start, block_size, 1)
    input_part = contract_rows(feature_block, activations)
    unit_levels = levels_of(block_size // hidden_own)
    grad_block = double_up(
        gradients,
        work_position,
        unit_levels,
        lambda pieces, degree: swapped(pieces, "work", degree),
        1,
    )
    output_part = contract_rows(grad_block, gradients)
    input_sum, output_factor = (
        lax.psum(input_part.astype(jnp.bfloat16), "dp").astype(jnp.float32),
        lax.psum(output_part.astype(jnp.bfloat16), "dp").astype(jnp.float32),
    )
    input_factor = input_sum / total_tokens
    grad_rows = lax.psum_scatter(
        contract_rows(whole_x, gradients), "dp", scatter_dimension=0, tiled=True
    )
    grad_wide = double_up(
        grad_rows,
        work_position,
        unit_levels,
        lambda pieces, degree: swapped(pieces.astype(jnp.bfloat16), "work", degree).astype(
            pieces.dtype
        ),
        1,
    )
    grad_upper, grad_lower = split_pair(grad_wide)
    right_prod = jnp.dot(grad_upper, right_inverse, preferred_element_type=jnp.float32) + jnp.dot(
        grad_lower, right_inverse, preferred_element_type=jnp.float32
    )
    right_side = right_prod.astype(jnp.bfloat16)
    right_block = double_up(
        right_side,
        data_position,
        levels_of(block_size // row_share),
        lambda pieces, degree: swapped(pieces, "dp", degree),
        0,
    )
    slots_held = left_panels.shape[0]
    panel_width = left_panels.shape[2]
    first_panel = data_position * row_share // panel_width
    columns_got = []
    for offset in range(row_share // panel_width):
        slot_index = panel_slot[first_panel + offset]
        stored = lax.dynamic_index_in_dim(left_panels, slot_index % slots_held, 0, keepdims=False)
        columns_got.append(spread(stored, "work", slot_index // slots_held))
    left_factor = jnp.concatenate(columns_got, 1)
    step_update = contract_rows(left_factor, right_block).astype(jnp.bfloat16)
    return (input_factor, output_factor, step_update)


def solution(mesh):
    return jax.shard_map(
        local,
        mesh=mesh,
        in_specs=(P("dp", "work"), P("dp", "work"), P("work", None, None), P(), P(None, "work")),
        out_specs=(P(None, "work"), P(None, "work"), P("dp", "work")),
        check_vma=False,
    )
```

profile of v0, /device:TPU:1, one launch (start us, length us, event | category | flops | bytes accessed | tf_op | source)
XLA Modules:
  0.0 880.6 jit_solution(2312969591638033345)
XLA Ops:
  7.2 0.0 copy-start
  7.2 0.0 all-gather.2.cloned.1.call-start
  7.2 0.7 all-gather.2.cloned.1.call-update
  7.9 0.0 reduce-scatter.2.cloned.1.call-start
  8.0 157.5 %all-gather.2.cloned.1.call-done = bf16[1024,4096]{1,0:T(8,128)(2,1)} async-done(((bf16[1024,128]{1,0:T(8,128)(2,1)}), bf16[1024,4096]{1,0:T(8,128)(2,1)}) %all-gather.2.cloned.1.call-update) | async-done | bytes 8388624 | tf_op jit(solution)/shard_map/all_gather | solution.py:57
  165.4 7.8 fusion.35
  173.3 0.0 copy-start.1
  173.3 0.0 reduce-scatter.2.cloned.1.call-update
  173.3 0.0 all-reduce.7.cloned.1.call-start
  173.3 1.0 copy-done.1
  174.3 2.1 collective-permute-start
  176.5 1.6 collective-permute-done
  178.1 0.2 maximum_select_fusion.4
  178.3 4.7 collective-permute-start.1
  183.1 0.0 copy-start.2
  183.1 79.1 %collective-permute-done.1 = bf16[1024,512]{1,0:T(8,128)(2,1)S(1)} collective-permute-done((bf16[1024,512]{1,0:T(8,128)(2,1)S(1)}, bf16[1024,512]{1,0:T(8,128)(2,1)S(1)}, u32[]{:S(2)}, u32[]{:S(2)}) %collective-permute-start.1) | collective-permute-done | bytes 1048608 | tf_op jit(solution)/shard_map/ppermute | solution.py:10
  262.2 1.6 fusion.9
  263.8 0.0 copy-done.2
  263.8 3.1 fusion.10
  266.8 0.0 copy-start.4
  266.8 0.0 all-reduce.7.cloned.1.call-update
  266.8 0.0 all-reduce.5.cloned.1.call-start
  266.9 75.6 %reduce-scatter.2.cloned.1.call-done = f32[256,256]{1,0:T(8,128)} async-done(((f32[4096,256]{1,0:T(8,128)}), f32[256,256]{1,0:T(8,128)}) %reduce-scatter.2.cloned.1.call-update) | async-done | bytes 262160 | tf_op jit(solution)/shard_map/reduce_scatter | solution.py:75
  342.5 1.0 convert_element_type.46
  343.5 2.3 collective-permute-start.2
  345.8 1.0 collective-permute-done.2
  346.8 1.1 fusion.33
  347.9 1.9 collective-permute-start.3
  349.9 0.0 copy-done.4
  349.9 0.7 fusion.34
  351.8 0.0 copy-done.3
  351.8 0.8 select_bitcast_fusion.1
  352.6 0.0 all-reduce.5.cloned.1.call-update
  352.7 22.7 %collective-permute-done.3 = bf16[256,512]{1,0:T(8,128)(2,1)S(1)} collective-permute-done((bf16[256,512]{1,0:T(8,128)(2,1)S(1)}, bf16[256,512]{1,0:T(8,128)(2,1)S(1)}, u32[]{:S(2)}, u32[]{:S(2)}) %collective-permute-start.3) | collective-permute-done | bytes 262176 | tf_op jit(solution)/shard_map/ppermute | solution.py:10
  375.3 0.1 convert_element_type.49
  375.4 0.0 copy-done
  375.4 0.3 fusion.26
  375.7 0.3 fusion.13
  376.0 1.9 collective-permute-start.4
  378.0 5.5 collective-permute-done.4
  383.4 0.1 maximum_select_fusion.9
  383.5 1.9 collective-permute-start.5
  385.5 130.0 %all-reduce.7.cloned.1.call-done = (bf16[1024,128]{1,0:T(8,128)(2,1)}, bf16[1024,256]{1,0:T(8,128)(2,1)}) async-done(((bf16[1024,128]{1,0:T(8,128)(2,1)}, bf16[1024,256]{1,0:T(8,128)(2,1)}), (bf16[1024,128]{1,0:T(8,128)(2,1)}, bf16[1024,256]{1,0:T(8,128)(2,1)})) %all-reduce.7.cloned.1.call-update) | async-done | bytes 786448 | tf_op jit(solution)/shard_map/psum | solution.py:71
  515.5 2.1 convert_element_type.45
  517.6 1.8 convert_multiply_fusion
  519.4 352.7 %all-reduce.5.cloned.1.call-done = (bf16[1024,128]{1,0:T(8,128)(2,1)}, bf16[1024,128]{1,0:T(8,128)(2,1)}) async-done(((bf16[1024,128]{1,0:T(8,128)(2,1)}, bf16[1024,128]{1,0:T(8,128)(2,1)}), (bf16[1024,128]{1,0:T(8,128)(2,1)}, bf16[1024,128]{1,0:T(8,128)(2,1)})) %all-reduce.5.cloned.1.call-update) | async-done | bytes 524304 | tf_op jit(solution)/shard_map/psum | solution.py:15
  872.0 0.0 collective-permute-done.5
  872.0 2.0 convolution_convert_fusion
  (2 shorter events, 0.0 us)
Async XLA Ops:
  7.2 368.2 %copy-start = (bf16[1024,256]{1,0:T(8,128)(2,1)S(1)}, bf16[1024,256]{1,0:T(8,128)(2,1)}, u32[]{:S(2)}) copy-start(bf16[1024,256]{1,0:T(8,128)(2,1)} %param.9) | copy-start | bytes 1572868
  7.2 158.2 %all-gather.2.cloned.1.call-start = ((), (), s32[]{:S(2)}) async-start(), calls=%async_computation.1 | async-start | bytes 8650752 | tf_op jit(solution)/shard_map/all_gather | solution.py:57
  7.9 334.6 %reduce-scatter.2.cloned.1.call-start = ((), (), s32[]{:S(2)}) async-start(), calls=%async_computation.2 | async-start | bytes 4456448 | tf_op jit(solution)/shard_map/reduce_scatter | solution.py:75
  173.3 1.0 copy-start.1
  173.3 342.2 %all-reduce.7.cloned.1.call-start = ((), (), s32[]{:S(2)}) async-start(), calls=%async_computation.4 | async-start | bytes 1572864 | tf_op jit(solution)/shard_map/psum | solution.py:71
  174.3 3.8 collective-permute-start
  178.3 83.8 %collective-permute-start.1 = (bf16[1024,512]{1,0:T(8,128)(2,1)S(1)}, bf16[1024,512]{1,0:T(8,128)(2,1)S(1)}, u32[]{:S(2)}, u32[]{:S(2)}) collective-permute-start(bf16[1024,512]{1,0:T(8,128)(2,1)S(1)} %maximum_select_fusion.4), channel_id=1, source_target_pairs={{0,2},{1,3},{2,0},{3,1},{4,6},{5,7},{6,4},{7,5},{8,10},{9,11},{10,... | collective-permute-start | bytes 3145736 | tf_op jit(solution)/shard_map/ppermute | solution.py:10
  183.1 80.6 %copy-start.2 = (bf16[1024,128]{1,0:T(8,128)(2,1)S(1)}, bf16[1024,128]{1,0:T(8,128)(2,1)}, u32[]{:S(2)}) copy-start(bf16[1024,128]{1,0:T(8,128)(2,1)} %param.5) | copy-start | bytes 786436
  266.8 83.1 %copy-start.4 = (s32[32]{0:T(128)S(1)}, s32[32]{0:T(128)}, u32[]{:S(2)}) copy-start(s32[32]{0:T(128)} %param.8) | copy-start | bytes 388
  266.8 85.0 %copy-start.3 = (bf16[1,1024,128]{2,1,0:T(8,128)(2,1)S(1)}, bf16[1,1024,128]{2,1,0:T(8,128)(2,1)}, u32[]{:S(2)}) copy-start(bf16[1,1024,128]{2,1,0:T(8,128)(2,1)} %param.7) | copy-start | bytes 786436
  266.8 605.2 %all-reduce.5.cloned.1.call-start = ((), (), s32[]{:S(2)}) async-start(), calls=%async_computation.3 | async-start | bytes 1048576 | tf_op jit(solution)/shard_map/psum | solution.py:15
  343.5 3.3 collective-permute-start.2
  347.9 27.4 %collective-permute-start.3 = (bf16[256,512]{1,0:T(8,128)(2,1)S(1)}, bf16[256,512]{1,0:T(8,128)(2,1)S(1)}, u32[]{:S(2)}, u32[]{:S(2)}) collective-permute-start(bf16[256,512]{1,0:T(8,128)(2,1)S(1)} %get-tuple-element.7), channel_id=1, source_target_pairs={{0,2},{1,3},{2,0},{3,1},{4,6},{5,7},{6,4},{7,5},{8,10},{9,11},{10,... | collective-permute-start | bytes 786440 | tf_op jit(solution)/shard_map/ppermute | solution.py:10
  376.0 7.4 collective-permute-start.4
  383.5 488.5 %collective-permute-start.5 = (bf16[512,256]{1,0:T(8,128)(2,1)S(1)}, bf16[512,256]{1,0:T(8,128)(2,1)S(1)}, u32[]{:S(2)}, u32[]{:S(2)}) collective-permute-start(bf16[512,256]{1,0:T(8,128)(2,1)S(1)} %maximum_select_fusion.9), channel_id=1, source_target_pairs={{0,64},{32,96},{64,0},{96,32},{128,192},{160,224},{192,128},{224,1... | collective-permute-start | bytes 786440 | tf_op jit(solution)/shard_map/ppermute | solution.py:10
Sparse Core Ops, SparseCore 0:
  11.1 154.3 all-gather.1
  173.4 169.0 reduce-scatter.1
  346.1 169.3 all-reduce.6
  518.6 353.4 all-reduce.4
where the time goes:
time: 881 us
  waiting for transfers between devices  826 us (94%)
  between operations  15.3 us (2%)
  starting transfers between devices  15.1 us (2%)
  matrix products  15.1 us (2%)
    psum x1, waiting for transfers between devices, spread(): return lax.psum(kept, axis)  353 us
    all_gather x1, waiting for transfers between devices, local(): whole_x = lax.all_gather(activations, 'work', axis=1, tiled=True)  157 us
    psum x1, waiting for transfers between devices, local(): lax.psum(input_part.astype(jnp.bfloat16), 'dp').astype(jnp.float32)  130 us
    ppermute x6, waiting for transfers between devices, swapped(): return lax.ppermute(value, axis, pairs)  110 us
    reduce_scatter x1, waiting for transfers between devices, local(): lax.psum_scatter(contract_rows(whole_x, gradients), 'dp', scatter_dimensi...  75.6 us
  transfers between devices with their start and end apart: 10, of which 9 were waited for; matrix products, arithmetic and copies ran while one was open for 1% of the time, Pallas kernels for 0%

commit v1 on v0

v1 whole, which is shorter than its diff:
```python
import jax
import jax.numpy as jnp
import numpy as np
from jax import lax
from jax.sharding import Mesh, PartitionSpec as P

BF16 = jnp.bfloat16
SHIFTS = (1, 2, 3)


def shifted(value, axis, shift):
    size = lax.axis_size(axis)
    return lax.ppermute(value, axis, [(i, (i + shift) % size) for i in range(size)])


def swapped(value, axis, mask):
    return lax.ppermute(value, axis, [(i, i ^ mask) for i in range(lax.axis_size(axis))])


def contract_rows(first_operand, second_operand):
    return lax.dot_general(
        first_operand, second_operand, (((0,), (0,)), ((), ())), preferred_element_type=jnp.float32
    )


def pick(stacked, index):
    return lax.dynamic_index_in_dim(stacked, index, 0, keepdims=False)


def contract_tokens(stacked, values):
    return jnp.einsum("btf,tc->bfc", stacked, values, preferred_element_type=jnp.float32)


def product(values, matrix):
    return jnp.dot(values, matrix, preferred_element_type=jnp.float32)


def block_order(values, place, levels):
    columns = values.shape[-1]
    values = values.reshape((2,) * levels + (-1, columns))
    for level in range(levels):
        flipped = jnp.flip(values, levels - 1 - level)
        values = jnp.where((place >> level) % 2 == 1, flipped, values)
    return values.reshape(-1, columns)


def together(*values):
    return lax.optimization_barrier(values)


def after(value, *others):
    return together(value, *others)[0]


def exchanged(pieces, axes):
    return lax.all_to_all(pieces, axes, 0, 0, tiled=True)


def to_all(value, axes, members):
    return exchanged(jnp.broadcast_to(value[None], (members,) + value.shape), axes)


def block_panels(side, panel_slot, h, k):
    rows, width = side.shape[1] // 8, side.shape[2]
    side = side.reshape(16, 2, rows, width)
    own = lax.dynamic_index_in_dim(side, k, 1, keepdims=False)
    other = swapped(lax.dynamic_index_in_dim(side, 1 - k, 1, keepdims=False), "k", 1)
    stored = jnp.concatenate([own, other], 0)
    at = (panel_slot // 2 ^ h) + 16 * ((panel_slot + k) % 2)
    ordered = jnp.take(stored, at, axis=0, mode="clip")
    return ordered.reshape(4, 8, rows, width)


def local(activations, gradients, left_panels, panel_slot, right_inverse):
    x, l, h, k = (lax.axis_index(name) for name in ("x", "l", "h", "k"))
    total_tokens = activations.shape[0] * 16
    tokens, width = gradients.shape
    own_width = activations.shape[1]
    place = 2 * (h % 2) + k

    panel = pick(left_panels.reshape(4, -1, own_width), x)
    act_0 = jnp.concatenate([activations, panel], 0)
    act_1 = swapped(act_0, "h", 1)
    act_3 = swapped(act_0, "h", 3)
    panel_2 = swapped(panel, "h", 2)
    act_1, act_3, panel_2, gradients = together(act_1, act_3, panel_2, gradients)
    act_2 = swapped(act_1[:tokens], "h", 3)
    grad_1 = swapped(gradients, "h", 1)
    panels = jnp.concatenate([panel, act_1[tokens:], panel_2, act_3[tokens:]], 0)
    mine = jnp.concatenate([activations, act_1[:tokens], act_3[:tokens], panels], 1)
    early = to_all(mine, "y", 4)
    grad_other = swapped(gradients, "k", 1)
    mine_other = swapped(mine, "k", 1)
    inverse = block_order(right_inverse, place, 2).reshape(4, width, -1)
    grad_right = product(gradients, inverse[0]) + product(grad_other, inverse[1])
    output_part = [contract_rows(gradients, gradients), contract_rows(grad_other, gradients)]
    input_part = [contract_rows(part, activations) for part in (mine, mine_other)]
    act_2, grad_1, early, grad_right, inverse, output_0, output_1, input_0, input_1 = together(
        act_2, grad_1, early, grad_right, inverse, *output_part, *input_part
    )

    third = to_all(act_2, "y", 4)
    grad_1_other = swapped(grad_1, "k", 1)
    grad_right = grad_right + product(grad_1, inverse[2]) + product(grad_1_other, inverse[3])
    grad_right = grad_right.astype(BF16)
    ordered = block_panels(early[..., 3 * own_width :], panel_slot, h, k)
    grad_right_other, ordered = together(swapped(grad_right, "k", 1), ordered)
    grad_right = jnp.concatenate([grad_right, grad_right_other], 1)

    terms = contract_tokens(early, grad_right)[:, : 3 * own_width]
    terms = jnp.concatenate([terms, contract_tokens(third, grad_right)], 1)
    terms, act_2, grad_1 = together(terms.astype(BF16), act_2, grad_1)
    got = exchanged(terms, "x")

    input_part = [
        jnp.concatenate([part[: 3 * own_width], contract_rows(last, activations)], 0)
        for part, last in ((input_0, act_2), (input_1, swapped(act_2, "k", 1)))
    ]
    input_part = jnp.stack([part.reshape(4, own_width, own_width) for part in input_part], 1)
    input_part = jnp.concatenate([input_part[:2], input_part[3:], input_part[2:3]], 0)
    input_part = block_order(input_part, 2 * h + k, 3)
    output_part = [output_0, output_1, contract_rows(grad_1, gradients)]
    output_part = jnp.stack(output_part + [contract_rows(grad_1_other, gradients)])
    output_part = block_order(output_part, place, 2)
    factors = jnp.concatenate([input_part, output_part], 1).astype(BF16)
    factors = factors.reshape(4, -1, factors.shape[1])
    quarter = pick(factors, l).astype(jnp.float32)
    for shift in SHIFTS:
        sent = pick(factors, (l + shift) % 4)
        quarter = quarter + shifted(sent, "l", shift).astype(jnp.float32)
    quarter = quarter.astype(BF16)

    rows_got = [pick(ordered, x)] + [shifted(pick(ordered, (x + s) % 4), "x", s) for s in SHIFTS]
    got, quarter, *rows_got = together(got, quarter, *rows_got)
    rows_got = jnp.stack(rows_got)
    left = jnp.concatenate([pick(rows_got, (x - (h ^ m)) % 4) for m in (0, 1, 3, 2)], 1)
    left_other = swapped(left, "k", 1)

    quarter = jnp.sum(to_all(quarter, "x", 4).astype(jnp.float32), 0).astype(BF16)
    right_rows = jnp.sum(got.astype(jnp.float32), 0).astype(BF16)
    right_other = swapped(right_rows[:, width:], "k", 1)
    update = contract_tokens(left, right_rows[:, :width]) + contract_tokens(left_other, right_other)
    update = update.astype(BF16).reshape(4, -1, width)
    quarter = jnp.broadcast_to(quarter[None], (4,) + quarter.shape)
    joint = exchanged(jnp.concatenate([update, quarter], 2), "l")
    step_update = jnp.sum(joint[..., :width].astype(jnp.float32), 0).astype(BF16)
    factors = joint[..., width:].reshape(-1, quarter.shape[2]).astype(jnp.float32)
    return factors[:, :own_width] / total_tokens, factors[:, own_width:], step_update


def solution(mesh):
    whole = Mesh(np.asarray(mesh.devices).reshape(4, 4, 4, 4, 2), ("x", "l", "y", "h", "k"))
    dp, work = ("x", "l"), ("y", "h", "k")
    return jax.shard_map(
        local,
        mesh=whole,
        in_specs=(P(dp, work), P(dp, work), P(work, None, None), P(), P(None, work)),
        out_specs=(P(None, work), P(None, work), P(dp, work)),
        check_vma=False,
    )
```

time: 881 us -> 265 us (0.30)
  waiting for transfers between devices: 826 us -> 82.2 us
  starting transfers between devices: 15.1 us -> 98.6 us
  blocking collectives: 0 us -> 33.3 us
  between operations: 15.3 us -> 1.68 us
  matrix products: 15.1 us -> 25.9 us
  local copies, waits for them, and re-layouts: 1.64 us -> 10.8 us
    psum x2 -> x0, waiting for transfers between devices: 483 us -> none  [the longest x1 353 us: spread(): return lax.psum(kept, axis)]
    all_gather x1 -> x0, waiting for transfers between devices: 157 us -> none  [local(): whole_x = lax.all_gather(activations, 'work', axis=1, tiled=True)]
    reduce_scatter x1 -> x0, waiting for transfers between devices: 75.6 us -> none  [local(): lax.psum_scatter(contract_rows(whole_x, gradients), 'dp', scatter_dimensi...]
    ppermute x6 -> x19, starting transfers between devices: 14.9 us -> 81.2 us  [the longest x13 63.3 us: swapped(): lax.ppermute(value, axis, [(i, i ^ mask) for i in range(lax.axis_size(axi...]
    ppermute x6 -> x19, waiting for transfers between devices: 110 us -> 70.3 us  [the longest x13 57 us: swapped(): lax.ppermute(value, axis, [(i, i ^ mask) for i in range(lax.axis_size(axi...]
    all_to_all x0 -> x1, blocking collectives: none -> 33.3 us  [exchanged(): return lax.all_to_all(pieces, axes, 0, 0, tiled=True)]
    all_to_all x0 -> x4, starting transfers between devices: none -> 17.5 us  [exchanged(): return lax.all_to_all(pieces, axes, 0, 0, tiled=True)]
    dot_general x2 -> x8, matrix products: 0.61 us -> 15.5 us  [the longest x4 11.5 us: contract_tokens(): jnp.einsum('btf,tc->bfc', stacked, values, preferred_element_type=jnp.flo...]
  transfers between devices with their start and end apart: 10 -> 23, of which waited for: 9 -> 10; matrix products, arithmetic and copies ran while one was open for 1% -> 13% of each run, Pallas kernels for 0% -> 0%
where the time goes in v1:
time: 265 us; the launch traced here: 263 us
  starting transfers between devices  98.6 us (37%)
  waiting for transfers between devices  82.2 us (31%)
  blocking collectives  33.3 us (13%)
  matrix products  25.9 us (10%)
  other arithmetic  10.9 us (4%)
  local copies, waits for them, and re-layouts  10.8 us (4%)
    ppermute x13, starting transfers between devices, swapped(): lax.ppermute(value, axis, [(i, i ^ mask) for i in range(lax.axis_size(axi...  63.3 us
    ppermute x13, waiting for transfers between devices, swapped(): lax.ppermute(value, axis, [(i, i ^ mask) for i in range(lax.axis_size(axi...  57 us
    all_to_all x1, blocking collectives, exchanged(): return lax.all_to_all(pieces, axes, 0, 0, tiled=True)  33.3 us
    ppermute x6, starting transfers between devices, shifted(): lax.ppermute(value, axis, [(i, (i + shift) % size) for i in range(size)])  17.9 us
    all_to_all x4, starting transfers between devices, exchanged(): return lax.all_to_all(pieces, axes, 0, 0, tiled=True)  17.5 us
    ppermute x6, waiting for transfers between devices, shifted(): lax.ppermute(value, axis, [(i, (i + shift) % size) for i in range(size)])  13.3 us
    all_to_all x4, waiting for transfers between devices, exchanged(): return lax.all_to_all(pieces, axes, 0, 0, tiled=True)  11.9 us
    dot_general x4, matrix products, contract_tokens(): jnp.einsum('btf,tc->bfc', stacked, values, preferred_element_type=jnp.flo...  11.5 us
  transfers between devices with their start and end apart: 23, of which 10 were waited for; matrix products, arithmetic and copies ran while one was open for 13% of the time, Pallas kernels for 0%

profile of v1, /device:TPU:1, one launch (start us, length us, event | category | flops | bytes accessed | tf_op | source)
XLA Modules:
  0.0 263.5 jit_solution(12751844181636422332)
XLA Ops:
  2.6 9.6 %collective-permute-start = (bf16[1280,128]{1,0:T(8,128)(2,1)S(1)}, bf16[1280,128]{1,0:T(8,128)(2,1)S(1)}, u32[]{:S(2)}, u32[]{:S(2)}) collective-permute-start(bf16[1280,128]{1,0:T(8,128)(2,1)S(1)} %pad_maximum_fusion.6), channel_id=1, source_target_pairs={{0,2},{2,0},{4,6},{6,4},{1,3},{3,1},{5,7},{7,5},{8,10},{10,8},{12,... | collective-permute-start | bytes 983048 | tf_op jit(solution)/shard_map/ppermute | solution.py:17
  12.2 8.8 %collective-permute-start.1 = (bf16[1280,128]{1,0:T(8,128)(2,1)S(1)}, bf16[1280,128]{1,0:T(8,128)(2,1)S(1)}, u32[]{:S(2)}, u32[]{:S(2)}) collective-permute-start(bf16[1280,128]{1,0:T(8,128)(2,1)S(1)} %pad_maximum_fusion.6), channel_id=1, source_target_pairs={{0,6},{2,4},{4,2},{6,0},{1,7},{3,5},{5,3},{7,1},{8,14},{10,12},{12... | collective-permute-start | bytes 983048 | tf_op jit(solution)/shard_map/ppermute | solution.py:17
  21.0 3.7 %collective-permute-start.2 = (bf16[256,128]{1,0:T(8,128)(2,1)S(1)}, bf16[256,128]{1,0:T(8,128)(2,1)S(1)}, u32[]{:S(2)}, u32[]{:S(2)}) collective-permute-start(bf16[256,128]{1,0:T(8,128)(2,1)S(1)} %dynamic-slice_bitcast_fusion.6), channel_id=1, source_target_pairs={{0,4},{2,6},{4,0},{6,2},{1,5},{3,7},{5,1},{7,3},{8,12},{10,14},{12... | collective-permute-start | bytes 196616 | tf_op jit(solution)/shard_map/ppermute | solution.py:17
  24.8 15.6 %collective-permute-done.2 = bf16[256,128]{1,0:T(8,128)(2,1)S(1)} collective-permute-done((bf16[256,128]{1,0:T(8,128)(2,1)S(1)}, bf16[256,128]{1,0:T(8,128)(2,1)S(1)}, u32[]{:S(2)}, u32[]{:S(2)}) %collective-permute-start.2) | collective-permute-done | bytes 65568 | tf_op jit(solution)/shard_map/ppermute | solution.py:17
  40.4 2.5 collective-permute-done
  44.0 2.4 broadcast_in_dim.12
  46.4 5.0 %all-to-all-start = ((bf16[4,1024,512]{2,1,0:T(8,128)(2,1)}), bf16[4,1024,512]{2,1,0:T(8,128)(2,1)}, u32[]{:S(2)}, u32[]{:S(2)}) async-start(bf16[4,1024,512]{2,1,0:T(8,128)(2,1)} %broadcast_in_dim.12), calls=%async_computation | async-start | bytes 8388608 | tf_op jit(solution)/shard_map/all_to_all | solution.py:56
  51.5 13.9 %collective-permute-start.5 = (bf16[1024,256]{1,0:T(8,128)(2,1)}, bf16[1024,256]{1,0:T(8,128)(2,1)S(1)}, u32[]{:S(2)}, u32[]{:S(2)}) collective-permute-start(bf16[1024,256]{1,0:T(8,128)(2,1)} %param.6), channel_id=1, source_target_pairs={{0,1},{1,0},{2,3},{3,2},{4,5},{5,4},{6,7},{7,6},{8,9},{9,8},{10,11... | collective-permute-start | bytes 1572872 | tf_op jit(solution)/shard_map/ppermute | solution.py:17
  65.5 8.7 %collective-permute-start.3 = (bf16[1024,128]{1,0:T(8,128)(2,1)S(1)}, bf16[1024,128]{1,0:T(8,128)(2,1)S(1)}, u32[]{:S(2)}, u32[]{:S(2)}) collective-permute-start(bf16[1024,128]{1,0:T(8,128)(2,1)S(1)} %slice.65), channel_id=1, source_target_pairs={{0,6},{2,4},{4,2},{6,0},{1,7},{3,5},{5,3},{7,1},{8,14},{10,12},{12... | collective-permute-start | bytes 786440 | tf_op jit(solution)/shard_map/ppermute | solution.py:17
  74.2 1.9 collective-permute-start.4
  76.2 2.2 collective-permute-start.6
  78.9 2.3 fusion.34
  81.5 1.3 convolution_add_fusion
  82.8 2.0 fusion.35
  86.0 7.2 %collective-permute-done.3 = bf16[1024,128]{1,0:T(8,128)(2,1)S(1)} collective-permute-done((bf16[1024,128]{1,0:T(8,128)(2,1)S(1)}, bf16[1024,128]{1,0:T(8,128)(2,1)S(1)}, u32[]{:S(2)}, u32[]{:S(2)}) %collective-permute-start.3) | collective-permute-done | bytes 262176 | tf_op jit(solution)/shard_map/ppermute | solution.py:17
  93.2 30.8 %collective-permute-done.4 = bf16[1024,256]{1,0:T(8,128)(2,1)} collective-permute-done((bf16[1024,256]{1,0:T(8,128)(2,1)}, bf16[1024,256]{1,0:T(8,128)(2,1)}, u32[]{:S(2)}, u32[]{:S(2)}) %collective-permute-start.4) | collective-permute-done | bytes 524320 | tf_op jit(solution)/shard_map/ppermute | solution.py:17
  124.0 2.4 collective-permute-start.7
  126.4 1.4 slice.73
  127.9 2.0 collective-permute-start.9
  129.9 1.3 fusion.25
  132.3 2.4 collective-permute-start.8
  136.1 4.4 %all-to-all-start.1 = ((bf16[4,1024,128]{1,2,0:T(8,128)(2,1)}), bf16[4,1024,128]{1,2,0:T(8,128)(2,1)}, u32[]{:S(2)}, u32[]{:S(2)}) async-start(bf16[4,1024,128]{1,2,0:T(8,128)(2,1)} %broadcast_in_dim.14), calls=%async_computation.1 | async-start | bytes 2097152 | tf_op jit(solution)/shard_map/all_to_all | solution.py:56
  140.5 1.2 pad_maximum_fusion.2
  142.4 1.4 convolution_bitcast_fusion
  143.9 4.8 %fusion.2 = bf16[4,512,512]{2,1,0:T(8,128)(2,1)S(1)} fusion(bf16[4,1024,512]{2,1,0:T(8,128)(2,1)} %all-to-all-done, bf16[1024,256]{1,0:T(8,128)(2,1)} %collective-permute-done.8, bf16[1024,256]{1,0:T(8,128)(2,1)} %add_convert_fusion), kind=kOutput, calls=%fused_computation.34 | convolution fusion | flops 2149580800 | bytes 7340032 | tf_op jit(solution)/shard_map/btf,tc->bfc/dot_general | solution.py:31
  148.8 6.7 %all-to-all-done.1 = bf16[4,1024,128]{1,2,0:T(8,128)(2,1)} async-done(((bf16[4,1024,128]{1,2,0:T(8,128)(2,1)}), bf16[4,1024,128]{1,2,0:T(8,128)(2,1)}, u32[]{:S(2)}, u32[]{:S(2)}) %all-to-all-start.1) | async-done | bytes 1048608 | tf_op jit(solution)/shard_map/all_to_all | solution.py:56
  155.5 2.2 convolution_convert_fusion
  157.7 1.5 pad_maximum_fusion
  159.2 3.0 %collective-permute-start.10 = (bf16[1024,128]{1,0:T(8,128)(2,1)S(1)}, bf16[1024,128]{1,0:T(8,128)(2,1)}, u32[]{:S(2)}, u32[]{:S(2)}) collective-permute-start(bf16[1024,128]{1,0:T(8,128)(2,1)S(1)} %collective-permute-done.3), channel_id=1, source_target_pairs={{0,1},{1,0},{2,3},{3,2},{4,5},{5,4},{6,7},{7,6},{8,9},{9,8},{10,11... | collective-permute-start | bytes 786440 | tf_op jit(solution)/shard_map/ppermute | solution.py:17
  162.5 4.6 %all-to-all-start.2 = ((bf16[4,512,512]{2,1,0:T(8,128)(2,1)}), bf16[4,512,512]{2,1,0:T(8,128)(2,1)}, u32[]{:S(2)}, u32[]{:S(2)}) async-start(bf16[4,512,512]{2,1,0:T(8,128)(2,1)} %pad_maximum_fusion), calls=%async_computation.2 | async-start | bytes 4194304 | tf_op jit(solution)/shard_map/all_to_all | solution.py:56
  167.1 1.6 convolution_bitcast_fusion.1
  169.1 1.2 fusion.39
  171.4 1.9 collective-permute-start.13
  173.4 1.9 collective-permute-start.12
  175.3 3.4 %collective-permute-start.11 = (bf16[256,384]{1,0:T(8,128)(2,1)S(1)}, bf16[256,384]{1,0:T(8,128)(2,1)}, u32[]{:S(2)}, u32[]{:S(2)}) collective-permute-start(bf16[256,384]{1,0:T(8,128)(2,1)S(1)} %get-tuple-element.61), channel_id=1, source_target_pairs={{0,32},{32,64},{64,96},{96,0},{1,33},{33,65},{65,97},{97,1},{2,34}... | collective-permute-start | bytes 589832 | tf_op jit(solution)/shard_map/ppermute | solution.py:13
  179.0 3.3 %collective-permute-start.14 = (bf16[8,128,128]{1,2,0:T(8,128)(2,1)S(1)}, bf16[8,128,128]{1,2,0:T(8,128)(2,1)S(1)}, u32[]{:S(2)}, u32[]{:S(2)}) collective-permute-start(bf16[8,128,128]{1,2,0:T(8,128)(2,1)S(1)} %bitcast.122), channel_id=1, source_target_pairs={{0,128},{128,256},{256,384},{384,0},{1,129},{129,257},{257,385},{3... | collective-permute-start | bytes 786440 | tf_op jit(solution)/shard_map/ppermute | solution.py:13
  182.5 4.3 %collective-permute-start.15 = (bf16[8,128,128]{1,2,0:T(8,128)(2,1)S(1)}, bf16[8,128,128]{1,2,0:T(8,128)(2,1)S(1)}, u32[]{:S(2)}, u32[]{:S(2)}) collective-permute-start(bf16[8,128,128]{1,2,0:T(8,128)(2,1)S(1)} %bitcast.123), channel_id=1, source_target_pairs={{0,256},{128,384},{256,0},{384,128},{1,257},{129,385},{257,1},{385... | collective-permute-start | bytes 786440 | tf_op jit(solution)/shard_map/ppermute | solution.py:13
  187.0 3.1 %collective-permute-start.16 = (bf16[8,128,128]{1,2,0:T(8,128)(2,1)S(1)}, bf16[8,128,128]{1,2,0:T(8,128)(2,1)S(1)}, u32[]{:S(2)}, u32[]{:S(2)}) collective-permute-start(bf16[8,128,128]{1,2,0:T(8,128)(2,1)S(1)} %bitcast.124), channel_id=1, source_target_pairs={{0,384},{128,0},{256,128},{384,256},{1,385},{129,1},{257,129},{385... | collective-permute-start | bytes 786440 | tf_op jit(solution)/shard_map/ppermute | solution.py:13
  192.6 7.1 %collective-permute-done.14 = bf16[8,128,128]{1,2,0:T(8,128)(2,1)S(1)} collective-permute-done((bf16[8,128,128]{1,2,0:T(8,128)(2,1)S(1)}, bf16[8,128,128]{1,2,0:T(8,128)(2,1)S(1)}, u32[]{:S(2)}, u32[]{:S(2)}) %collective-permute-start.14) | collective-permute-done | bytes 262176 | tf_op jit(solution)/shard_map/ppermute | solution.py:13
  199.7 5.1 %collective-permute-done.15 = bf16[8,128,128]{1,2,0:T(8,128)(2,1)S(1)} collective-permute-done((bf16[8,128,128]{1,2,0:T(8,128)(2,1)S(1)}, bf16[8,128,128]{1,2,0:T(8,128)(2,1)S(1)}, u32[]{:S(2)}, u32[]{:S(2)}) %collective-permute-start.15) | collective-permute-done | bytes 262176 | tf_op jit(solution)/shard_map/ppermute | solution.py:13
  205.2 2.7 %collective-permute-start.17 = (bf16[8,512,128]{1,2,0:T(8,128)(2,1)S(1)}, bf16[8,512,128]{1,2,0:T(8,128)(2,1)}, u32[]{:S(2)}, u32[]{:S(2)}) collective-permute-start(bf16[8,512,128]{1,2,0:T(8,128)(2,1)S(1)} %pad_maximum_fusion.5), channel_id=1, source_target_pairs={{0,1},{1,0},{2,3},{3,2},{4,5},{5,4},{6,7},{7,6},{8,9},{9,8},{10,11... | collective-permute-start | bytes 3145736 | tf_op jit(solution)/shard_map/ppermute | solution.py:17
  208.9 3.5 %all-to-all-start.3 = ((bf16[4,256,384]{2,1,0:T(8,128)(2,1)}), bf16[4,256,384]{2,1,0:T(8,128)(2,1)S(1)}, u32[]{:S(2)}, u32[]{:S(2)}) async-start(bf16[4,256,384]{2,1,0:T(8,128)(2,1)} %broadcast_in_dim.15), calls=%async_computation.3 | async-start | bytes 1572864 | tf_op jit(solution)/shard_map/all_to_all | solution.py:56
  212.4 2.2 reduce_sum.36
  215.3 1.9 collective-permute-start.18
  217.2 2.4 fusion.9
  219.6 5.2 %all-to-all-done.3 = bf16[4,256,384]{2,1,0:T(8,128)(2,1)S(1)} async-done(((bf16[4,256,384]{2,1,0:T(8,128)(2,1)}), bf16[4,256,384]{2,1,0:T(8,128)(2,1)S(1)}, u32[]{:S(2)}, u32[]{:S(2)}) %all-to-all-start.3) | async-done | bytes 786464 | tf_op jit(solution)/shard_map/all_to_all | solution.py:56
  225.0 2.1 fusion
  227.3 33.3 %all_to_all.25 = bf16[4,256,640]{2,1,0:T(8,128)(2,1)S(1)} all-to-all(bf16[4,256,640]{2,1,0:T(8,128)(2,1)S(1)} %pad_maximum_fusion.1), channel_id=1, replica_groups=mesh['x'=4,'l'=4,'y'=4,'h'=4,'k'=2] {'l'}, dimensions={0} | all-to-all | bytes 2621440 | tf_op jit(solution)/shard_map/all_to_all | solution.py:56
  (96 shorter events, 18.4 us)
Async XLA Ops:
  0.6 1.0 copy-start
  0.6 43.2 %copy-start.1 = (bf16[1024,128]{1,0:T(8,128)(2,1)S(1)}, bf16[1024,128]{1,0:T(8,128)(2,1)}, u32[]{:S(2)}) copy-start(bf16[1024,128]{1,0:T(8,128)(2,1)} %param.5) | copy-start | bytes 786436
  2.6 40.4 %collective-permute-start = (bf16[1280,128]{1,0:T(8,128)(2,1)S(1)}, bf16[1280,128]{1,0:T(8,128)(2,1)S(1)}, u32[]{:S(2)}, u32[]{:S(2)}) collective-permute-start(bf16[1280,128]{1,0:T(8,128)(2,1)S(1)} %pad_maximum_fusion.6), channel_id=1, source_target_pairs={{0,2},{2,0},{4,6},{6,4},{1,3},{3,1},{5,7},{7,5},{8,10},{10,8},{12,... | collective-permute-start | bytes 983048 | tf_op jit(solution)/shard_map/ppermute | solution.py:17
  12.2 31.6 %collective-permute-start.1 = (bf16[1280,128]{1,0:T(8,128)(2,1)S(1)}, bf16[1280,128]{1,0:T(8,128)(2,1)S(1)}, u32[]{:S(2)}, u32[]{:S(2)}) collective-permute-start(bf16[1280,128]{1,0:T(8,128)(2,1)S(1)} %pad_maximum_fusion.6), channel_id=1, source_target_pairs={{0,6},{2,4},{4,2},{6,0},{1,7},{3,5},{5,3},{7,1},{8,14},{10,12},{12... | collective-permute-start | bytes 983048 | tf_op jit(solution)/shard_map/ppermute | solution.py:17
  21.0 19.3 %collective-permute-start.2 = (bf16[256,128]{1,0:T(8,128)(2,1)S(1)}, bf16[256,128]{1,0:T(8,128)(2,1)S(1)}, u32[]{:S(2)}, u32[]{:S(2)}) collective-permute-start(bf16[256,128]{1,0:T(8,128)(2,1)S(1)} %dynamic-slice_bitcast_fusion.6), channel_id=1, source_target_pairs={{0,4},{2,6},{4,0},{6,2},{1,5},{3,7},{5,1},{7,3},{8,12},{10,14},{12... | collective-permute-start | bytes 196616 | tf_op jit(solution)/shard_map/ppermute | solution.py:17
  46.4 5.0 %copy-start.7 = (bf16[1024,256]{1,0:T(8,128)(2,1)S(1)}, bf16[1024,256]{1,0:T(8,128)(2,1)}, u32[]{:S(2)}) copy-start(bf16[1024,256]{1,0:T(8,128)(2,1)} %param.9) | copy-start | bytes 1572868
  46.4 77.6 %all-to-all-start = ((bf16[4,1024,512]{2,1,0:T(8,128)(2,1)}), bf16[4,1024,512]{2,1,0:T(8,128)(2,1)}, u32[]{:S(2)}, u32[]{:S(2)}) async-start(bf16[4,1024,512]{2,1,0:T(8,128)(2,1)} %broadcast_in_dim.12), calls=%async_computation | async-start | bytes 8388608 | tf_op jit(solution)/shard_map/all_to_all | solution.py:56
  51.5 29.6 %collective-permute-start.5 = (bf16[1024,256]{1,0:T(8,128)(2,1)}, bf16[1024,256]{1,0:T(8,128)(2,1)S(1)}, u32[]{:S(2)}, u32[]{:S(2)}) collective-permute-start(bf16[1024,256]{1,0:T(8,128)(2,1)} %param.6), channel_id=1, source_target_pairs={{0,1},{1,0},{2,3},{3,2},{4,5},{5,4},{6,7},{7,6},{8,9},{9,8},{10,11... | collective-permute-start | bytes 1572872 | tf_op jit(solution)/shard_map/ppermute | solution.py:17
  65.5 16.0 %copy-start.2 = (bf16[2,2,256,256]{3,2,1,0:T(8,128)(2,1)}, bf16[2,2,256,256]{3,2,1,0:T(8,128)(2,1)S(1)}, u32[]{:S(2)}) copy-start(bf16[2,2,256,256]{3,2,1,0:T(8,128)(2,1)S(1)} %reverse_select_fusion.5) | copy-start | bytes 1572868
  65.5 27.7 %collective-permute-start.3 = (bf16[1024,128]{1,0:T(8,128)(2,1)S(1)}, bf16[1024,128]{1,0:T(8,128)(2,1)S(1)}, u32[]{:S(2)}, u32[]{:S(2)}) collective-permute-start(bf16[1024,128]{1,0:T(8,128)(2,1)S(1)} %slice.65), channel_id=1, source_target_pairs={{0,6},{2,4},{4,2},{6,0},{1,7},{3,5},{5,3},{7,1},{8,14},{10,12},{12... | collective-permute-start | bytes 786440 | tf_op jit(solution)/shard_map/ppermute | solution.py:17
  74.2 49.8 %collective-permute-start.4 = (bf16[1024,256]{1,0:T(8,128)(2,1)}, bf16[1024,256]{1,0:T(8,128)(2,1)}, u32[]{:S(2)}, u32[]{:S(2)}) collective-permute-start(bf16[1024,256]{1,0:T(8,128)(2,1)} %param.6), channel_id=1, source_target_pairs={{0,2},{2,0},{4,6},{6,4},{1,3},{3,1},{5,7},{7,5},{8,10},{10,8},{12,... | collective-permute-start | bytes 1572872 | tf_op jit(solution)/shard_map/ppermute | solution.py:17
  76.2 8.7 %collective-permute-start.6 = (bf16[1024,512]{1,0:T(8,128)(2,1)S(1)}, bf16[1024,512]{1,0:T(8,128)(2,1)S(1)}, u32[]{:S(2)}, u32[]{:S(2)}) collective-permute-start(bf16[1024,512]{1,0:T(8,128)(2,1)S(1)} %maximum_maximum_fusion), channel_id=1, source_target_pairs={{0,1},{1,0},{2,3},{3,2},{4,5},{5,4},{6,7},{7,6},{8,9},{9,8},{10,11... | collective-permute-start | bytes 3145736 | tf_op jit(solution)/shard_map/ppermute | solution.py:17
  78.9 61.6 %copy-start.8 = (bf16[512,128]{1,0:T(8,128)(2,1)}, bf16[512,128]{1,0:T(8,128)(2,1)S(1)}, u32[]{:S(2)}) copy-start(bf16[512,128]{1,0:T(8,128)(2,1)S(1)} %fusion.36) | copy-start | bytes 393220
  124.0 7.2 %collective-permute-start.7 = (bf16[1024,256]{1,0:T(8,128)(2,1)}, bf16[1024,256]{1,0:T(8,128)(2,1)S(1)}, u32[]{:S(2)}, u32[]{:S(2)}) collective-permute-start(bf16[1024,256]{1,0:T(8,128)(2,1)} %collective-permute-done.4), channel_id=1, source_target_pairs={{0,1},{1,0},{2,3},{3,2},{4,5},{5,4},{6,7},{7,6},{8,9},{9,8},{10,11... | collective-permute-start | bytes 1572872 | tf_op jit(solution)/shard_map/ppermute | solution.py:17
  126.4 3.5 %copy-start.3 = (bf16[2,2,256,256]{3,2,1,0:T(8,128)(2,1)S(1)}, bf16[2,2,256,256]{3,2,1,0:T(8,128)(2,1)}, u32[]{:S(2)}) copy-start(bf16[2,2,256,256]{3,2,1,0:T(8,128)(2,1)} %copy-done.2) | copy-start | bytes 1572868
  127.9 6.8 %copy-start.11 = (s32[32]{0:T(128)S(1)}, s32[32]{0:T(128)}, u32[]{:S(2)}) copy-start(s32[32]{0:T(128)} %param.8) | copy-start | bytes 388
  127.9 12.6 %collective-permute-start.9 = (bf16[16,128,128]{2,1,0:T(8,128)(2,1)S(1)}, bf16[16,128,128]{2,1,0:T(8,128)(2,1)}, u32[]{:S(2)}, u32[]{:S(2)}) collective-permute-start(bf16[16,128,128]{2,1,0:T(8,128)(2,1)S(1)} %get-tuple-element.60), channel_id=1, source_target_pairs={{0,1},{1,0},{2,3},{3,2},{4,5},{5,4},{6,7},{7,6},{8,9},{9,8},{10,11... | collective-permute-start | bytes 1572872 | tf_op jit(solution)/shard_map/ppermute | solution.py:17
  131.2 3.6 %copy-start.5 = (bf16[1024,256]{1,0:T(8,128)(2,1)}, bf16[1024,256]{1,0:T(8,128)(2,1)S(1)}, u32[]{:S(2)}) copy-start(bf16[1024,256]{1,0:T(8,128)(2,1)S(1)} %collective-permute-done.7) | copy-start | bytes 1572868
  132.3 11.5 %collective-permute-start.8 = (bf16[1024,256]{1,0:T(8,128)(2,1)}, bf16[1024,256]{1,0:T(8,128)(2,1)}, u32[]{:S(2)}, u32[]{:S(2)}) collective-permute-start(bf16[1024,256]{1,0:T(8,128)(2,1)} %add_convert_fusion), channel_id=1, source_target_pairs={{0,1},{1,0},{2,3},{3,2},{4,5},{5,4},{6,7},{7,6},{8,9},{9,8},{10,11... | collective-permute-start | bytes 1572872 | tf_op jit(solution)/shard_map/ppermute | solution.py:17
  136.1 19.4 %all-to-all-start.1 = ((bf16[4,1024,128]{1,2,0:T(8,128)(2,1)}), bf16[4,1024,128]{1,2,0:T(8,128)(2,1)}, u32[]{:S(2)}, u32[]{:S(2)}) async-start(bf16[4,1024,128]{1,2,0:T(8,128)(2,1)} %broadcast_in_dim.14), calls=%async_computation.1 | async-start | bytes 2097152 | tf_op jit(solution)/shard_map/all_to_all | solution.py:56
  140.5 2.0 copy-start.6
  159.2 9.9 %collective-permute-start.10 = (bf16[1024,128]{1,0:T(8,128)(2,1)S(1)}, bf16[1024,128]{1,0:T(8,128)(2,1)}, u32[]{:S(2)}, u32[]{:S(2)}) collective-permute-start(bf16[1024,128]{1,0:T(8,128)(2,1)S(1)} %collective-permute-done.3), channel_id=1, source_target_pairs={{0,1},{1,0},{2,3},{3,2},{4,5},{5,4},{6,7},{7,6},{8,9},{9,8},{10,11... | collective-permute-start | bytes 786440 | tf_op jit(solution)/shard_map/ppermute | solution.py:17
  162.5 6.2 %copy-start.9 = (bf16[256,256]{1,0:T(8,128)(2,1)S(1)}, bf16[256,256]{1,0:T(8,128)(2,1)}, u32[]{:S(2)}) copy-start(bf16[256,256]{1,0:T(8,128)(2,1)} %fusion.34) | copy-start | bytes 393220
  162.5 6.2 %copy-start.10 = (bf16[256,256]{1,0:T(8,128)(2,1)S(1)}, bf16[256,256]{1,0:T(8,128)(2,1)}, u32[]{:S(2)}) copy-start(bf16[256,256]{1,0:T(8,128)(2,1)} %fusion.35) | copy-start | bytes 393220
  162.5 42.3 %all-to-all-start.2 = ((bf16[4,512,512]{2,1,0:T(8,128)(2,1)}), bf16[4,512,512]{2,1,0:T(8,128)(2,1)}, u32[]{:S(2)}, u32[]{:S(2)}) async-start(bf16[4,512,512]{2,1,0:T(8,128)(2,1)} %pad_maximum_fusion), calls=%async_computation.2 | async-start | bytes 4194304 | tf_op jit(solution)/shard_map/all_to_all | solution.py:56
  167.1 1.8 slice-start
  168.7 1.6 slice-start.1
  171.4 15.6 %collective-permute-start.13 = (bf16[256,384]{1,0:T(8,128)(2,1)}, bf16[256,384]{1,0:T(8,128)(2,1)S(1)}, u32[]{:S(2)}, u32[]{:S(2)}) collective-permute-start(bf16[256,384]{1,0:T(8,128)(2,1)} %get-tuple-element.63), channel_id=1, source_target_pairs={{0,96},{32,0},{64,32},{96,64},{1,97},{33,1},{65,33},{97,65},{2,98}... | collective-permute-start | bytes 589832 | tf_op jit(solution)/shard_map/ppermute | solution.py:13
  173.4 18.1 %collective-permute-start.12 = (bf16[256,384]{1,0:T(8,128)(2,1)}, bf16[256,384]{1,0:T(8,128)(2,1)}, u32[]{:S(2)}, u32[]{:S(2)}) collective-permute-start(bf16[256,384]{1,0:T(8,128)(2,1)} %get-tuple-element.62), channel_id=1, source_target_pairs={{0,64},{32,96},{64,0},{96,32},{1,65},{33,97},{65,1},{97,33},{2,66}... | collective-permute-start | bytes 589832 | tf_op jit(solution)/shard_map/ppermute | solution.py:13
  175.3 16.2 %collective-permute-start.11 = (bf16[256,384]{1,0:T(8,128)(2,1)S(1)}, bf16[256,384]{1,0:T(8,128)(2,1)}, u32[]{:S(2)}, u32[]{:S(2)}) collective-permute-start(bf16[256,384]{1,0:T(8,128)(2,1)S(1)} %get-tuple-element.61), channel_id=1, source_target_pairs={{0,32},{32,64},{64,96},{96,0},{1,33},{33,65},{65,97},{97,1},{2,34}... | collective-permute-start | bytes 589832 | tf_op jit(solution)/shard_map/ppermute | solution.py:13
  179.0 20.7 %collective-permute-start.14 = (bf16[8,128,128]{1,2,0:T(8,128)(2,1)S(1)}, bf16[8,128,128]{1,2,0:T(8,128)(2,1)S(1)}, u32[]{:S(2)}, u32[]{:S(2)}) collective-permute-start(bf16[8,128,128]{1,2,0:T(8,128)(2,1)S(1)} %bitcast.122), channel_id=1, source_target_pairs={{0,128},{128,256},{256,384},{384,0},{1,129},{129,257},{257,385},{3... | collective-permute-start | bytes 786440 | tf_op jit(solution)/shard_map/ppermute | solution.py:13
  182.5 22.3 %collective-permute-start.15 = (bf16[8,128,128]{1,2,0:T(8,128)(2,1)S(1)}, bf16[8,128,128]{1,2,0:T(8,128)(2,1)S(1)}, u32[]{:S(2)}, u32[]{:S(2)}) collective-permute-start(bf16[8,128,128]{1,2,0:T(8,128)(2,1)S(1)} %bitcast.123), channel_id=1, source_target_pairs={{0,256},{128,384},{256,0},{384,128},{1,257},{129,385},{257,1},{385... | collective-permute-start | bytes 786440 | tf_op jit(solution)/shard_map/ppermute | solution.py:13
  187.0 17.8 %collective-permute-start.16 = (bf16[8,128,128]{1,2,0:T(8,128)(2,1)S(1)}, bf16[8,128,128]{1,2,0:T(8,128)(2,1)S(1)}, u32[]{:S(2)}, u32[]{:S(2)}) collective-permute-start(bf16[8,128,128]{1,2,0:T(8,128)(2,1)S(1)} %bitcast.124), channel_id=1, source_target_pairs={{0,384},{128,0},{256,128},{384,256},{1,385},{129,1},{257,129},{385... | collective-permute-start | bytes 786440 | tf_op jit(solution)/shard_map/ppermute | solution.py:13
  205.1 2.9 %copy-start.4 = (bf16[8,128,128]{1,2,0:T(8,128)(2,1)}, bf16[8,128,128]{1,2,0:T(8,128)(2,1)S(1)}, u32[]{:S(2)}) copy-start(bf16[8,128,128]{1,2,0:T(8,128)(2,1)S(1)} %get-tuple-element.54) | copy-start | bytes 786436
  205.2 19.8 %collective-permute-start.17 = (bf16[8,512,128]{1,2,0:T(8,128)(2,1)S(1)}, bf16[8,512,128]{1,2,0:T(8,128)(2,1)}, u32[]{:S(2)}, u32[]{:S(2)}) collective-permute-start(bf16[8,512,128]{1,2,0:T(8,128)(2,1)S(1)} %pad_maximum_fusion.5), channel_id=1, source_target_pairs={{0,1},{1,0},{2,3},{3,2},{4,5},{5,4},{6,7},{7,6},{8,9},{9,8},{10,11... | collective-permute-start | bytes 3145736 | tf_op jit(solution)/shard_map/ppermute | solution.py:17
  208.9 15.9 %all-to-all-start.3 = ((bf16[4,256,384]{2,1,0:T(8,128)(2,1)}), bf16[4,256,384]{2,1,0:T(8,128)(2,1)S(1)}, u32[]{:S(2)}, u32[]{:S(2)}) async-start(bf16[4,256,384]{2,1,0:T(8,128)(2,1)} %broadcast_in_dim.15), calls=%async_computation.3 | async-start | bytes 1572864 | tf_op jit(solution)/shard_map/all_to_all | solution.py:56
  215.3 9.7 %collective-permute-start.18 = (bf16[512,256]{1,0:T(8,128)(2,1)}, bf16[512,256]{1,0:T(8,128)(2,1)}, u32[]{:S(2)}, u32[]{:S(2)}) collective-permute-start(bf16[512,256]{1,0:T(8,128)(2,1)} %slice.96), channel_id=1, source_target_pairs={{0,1},{1,0},{2,3},{3,2},{4,5},{5,4},{6,7},{7,6},{8,9},{9,8},{10,11... | collective-permute-start | bytes 786440 | tf_op jit(solution)/shard_map/ppermute | solution.py:17

commit v2 on v1

--- a/solution.py
+++ b/solution.py
@@ -82,11 +82,10 @@
     act_0 = jnp.concatenate([activations, panel], 0)
     act_1 = swapped(act_0, "h", 1)
     act_3 = swapped(act_0, "h", 3)
-    panel_2 = swapped(panel, "h", 2)
-    act_1, act_3, panel_2, gradients = together(act_1, act_3, panel_2, gradients)
-    act_2 = swapped(act_1[:tokens], "h", 3)
+    act_1, act_3, gradients = together(act_1, act_3, gradients)
+    act_2 = swapped(act_1, "h", 3)
     grad_1 = swapped(gradients, "h", 1)
-    panels = jnp.concatenate([panel, act_1[tokens:], panel_2, act_3[tokens:]], 0)
+    panels = jnp.concatenate([panel, act_1[tokens:], panel, act_3[tokens:]], 0)
     mine = jnp.concatenate([activations, act_1[:tokens], act_3[:tokens], panels], 1)
     early = to_all(mine, "y", 4)
     grad_other = swapped(gradients, "k", 1)
@@ -103,13 +102,13 @@
     grad_1_other = swapped(grad_1, "k", 1)
     grad_right = grad_right + product(grad_1, inverse[2]) + product(grad_1_other, inverse[3])
     grad_right = grad_right.astype(BF16)
-    ordered = block_panels(early[..., 3 * own_width :], panel_slot, h, k)
-    grad_right_other, ordered = together(swapped(grad_right, "k", 1), ordered)
-    grad_right = jnp.concatenate([grad_right, grad_right_other], 1)
+    grad_right = jnp.concatenate([grad_right, swapped(grad_right, "k", 1)], 1)
 
     terms = contract_tokens(early, grad_right)[:, : 3 * own_width]
-    terms = jnp.concatenate([terms, contract_tokens(third, grad_right)], 1)
-    terms, act_2, grad_1 = together(terms.astype(BF16), act_2, grad_1)
+    terms = jnp.concatenate([terms, contract_tokens(third[:, :tokens], grad_right)], 1)
+    terms, act_2, grad_1, early, third = together(
+        terms.astype(BF16), act_2[:tokens], grad_1, early, third
+    )
     got = exchanged(terms, "x")
 
     input_part = [
@@ -130,6 +129,10 @@
         quarter = quarter + shifted(sent, "l", shift).astype(jnp.float32)
     quarter = quarter.astype(BF16)
 
+    held = panel.shape[0]
+    side = early[..., 3 * own_width :]
+    side = jnp.concatenate([side[:, : 2 * held], third[:, tokens:], side[:, 3 * held :]], 1)
+    ordered = block_panels(side, panel_slot, h, k)
     rows_got = [pick(ordered, x)] + [shifted(pick(ordered, (x + s) % 4), "x", s) for s in SHIFTS]
     got, quarter, *rows_got = together(got, quarter, *rows_got)
     rows_got = jnp.stack(rows_got)

time: 265 us -> 262 us (0.989)
  starting transfers between devices: 98.6 us -> 86.9 us
  waiting for transfers between devices: 82.2 us -> 86.6 us
  local copies, waits for them, and re-layouts: 10.8 us -> 14.4 us
    ppermute x13 -> x12, starting transfers between devices: 63.3 us -> 49.5 us  [swapped(): lax.ppermute(value, axis, [(i, i ^ mask) for i in range(lax.axis_size(axi...]
    ppermute x13 -> x12, waiting for transfers between devices: 57 us -> 63.4 us  [swapped(): lax.ppermute(value, axis, [(i, i ^ mask) for i in range(lax.axis_size(axi...]
    ppermute x6, waiting for transfers between devices: 13.3 us -> 8.07 us  [shifted(): lax.ppermute(value, axis, [(i, (i + shift) % size) for i in range(size)])]
    slice x4 -> x8, local copies, waits for them, and re-layouts: 1.39 us -> 4.83 us  [the longest x1 1.12 us: local(): side[:, :2 * held]]
    all_to_all x4, waiting for transfers between devices: 11.9 us -> 15.1 us  [exchanged(): return lax.all_to_all(pieces, axes, 0, 0, tiled=True)]
  transfers between devices with their start and end apart: 23 -> 22, of which waited for: 10 -> 9; matrix products, arithmetic and copies ran while one was open for 13% -> 12% of each run, Pallas kernels for 0% -> 0%
where the time goes in v2:
time: 262 us; the launch traced here: 260 us
  starting transfers between devices  86.9 us (33%)
  waiting for transfers between devices  86.6 us (33%)
  blocking collectives  33.3 us (13%)
  matrix products  27.8 us (11%)
  local copies, waits for them, and re-layouts  14.4 us (5%)
  other arithmetic  9.9 us (4%)
    ppermute x12, waiting for transfers between devices, swapped(): lax.ppermute(value, axis, [(i, i ^ mask) for i in range(lax.axis_size(axi...  63.4 us
    ppermute x12, starting transfers between devices, swapped(): lax.ppermute(value, axis, [(i, i ^ mask) for i in range(lax.axis_size(axi...  49.5 us
    all_to_all x1, blocking collectives, exchanged(): return lax.all_to_all(pieces, axes, 0, 0, tiled=True)  33.3 us
    ppermute x6, starting transfers between devices, shifted(): lax.ppermute(value, axis, [(i, (i + shift) % size) for i in range(size)])  20 us
    all_to_all x4, starting transfers between devices, exchanged(): return lax.all_to_all(pieces, axes, 0, 0, tiled=True)  17.5 us
    all_to_all x4, waiting for transfers between devices, exchanged(): return lax.all_to_all(pieces, axes, 0, 0, tiled=True)  15.1 us
    dot_general x8, matrix products, contract_rows(): lax.dot_general(first_operand, second_operand, (((0,), (0,)), ((), ())),...  12.6 us
    dot_general x4, matrix products, contract_tokens(): jnp.einsum('btf,tc->bfc', stacked, values, preferred_element_type=jnp.flo...  11.2 us
  transfers between devices with their start and end apart: 22, of which 9 were waited for; matrix products, arithmetic and copies ran while one was open for 12% of the time, Pallas kernels for 0%

profile of v2, /device:TPU:1, one launch (start us, length us, event | category | flops | bytes accessed | tf_op | source)
XLA Modules:
  0.0 260.5 jit_solution(16783282143051618410)
XLA Ops:
  2.6 13.3 %collective-permute-start.1 = (bf16[1280,128]{1,0:T(8,128)(2,1)S(1)}, bf16[1280,128]{1,0:T(8,128)(2,1)S(1)}, u32[]{:S(2)}, u32[]{:S(2)}) collective-permute-start(bf16[1280,128]{1,0:T(8,128)(2,1)S(1)} %pad_maximum_fusion.7), channel_id=1, source_target_pairs={{0,6},{2,4},{4,2},{6,0},{1,7},{3,5},{5,3},{7,1},{8,14},{10,12},{12... | collective-permute-start | bytes 983048 | tf_op jit(solution)/shard_map/ppermute | solution.py:17
  15.9 5.2 %collective-permute-start = (bf16[1280,128]{1,0:T(8,128)(2,1)S(1)}, bf16[1280,128]{1,0:T(8,128)(2,1)}, u32[]{:S(2)}, u32[]{:S(2)}) collective-permute-start(bf16[1280,128]{1,0:T(8,128)(2,1)S(1)} %pad_maximum_fusion.7), channel_id=1, source_target_pairs={{0,2},{2,0},{4,6},{6,4},{1,3},{3,1},{5,7},{7,5},{8,10},{10,8},{12,... | collective-permute-start | bytes 983048 | tf_op jit(solution)/shard_map/ppermute | solution.py:17
  21.0 22.9 %collective-permute-done.1 = bf16[1280,128]{1,0:T(8,128)(2,1)S(1)} collective-permute-done((bf16[1280,128]{1,0:T(8,128)(2,1)S(1)}, bf16[1280,128]{1,0:T(8,128)(2,1)S(1)}, u32[]{:S(2)}, u32[]{:S(2)}) %collective-permute-start.1) | collective-permute-done | bytes 327712 | tf_op jit(solution)/shard_map/ppermute | solution.py:17
  43.9 3.9 %collective-permute-done = bf16[1280,128]{1,0:T(8,128)(2,1)} collective-permute-done((bf16[1280,128]{1,0:T(8,128)(2,1)S(1)}, bf16[1280,128]{1,0:T(8,128)(2,1)}, u32[]{:S(2)}, u32[]{:S(2)}) %collective-permute-start) | collective-permute-done | bytes 327712 | tf_op jit(solution)/shard_map/ppermute | solution.py:17
  49.8 2.4 broadcast_in_dim.12
  52.2 5.0 %all-to-all-start = ((bf16[4,1024,512]{2,1,0:T(8,128)(2,1)}), bf16[4,1024,512]{2,1,0:T(8,128)(2,1)}, u32[]{:S(2)}, u32[]{:S(2)}) async-start(bf16[4,1024,512]{2,1,0:T(8,128)(2,1)} %broadcast_in_dim.12), calls=%async_computation | async-start | bytes 8388608 | tf_op jit(solution)/shard_map/all_to_all | solution.py:56
  57.3 2.9 %collective-permute-start.4 = (bf16[1024,256]{1,0:T(8,128)(2,1)}, bf16[1024,256]{1,0:T(8,128)(2,1)S(1)}, u32[]{:S(2)}, u32[]{:S(2)}) collective-permute-start(bf16[1024,256]{1,0:T(8,128)(2,1)} %param.6), channel_id=1, source_target_pairs={{0,1},{1,0},{2,3},{3,2},{4,5},{5,4},{6,7},{7,6},{8,9},{9,8},{10,11... | collective-permute-start | bytes 1572872 | tf_op jit(solution)/shard_map/ppermute | solution.py:17
  60.3 4.1 %collective-permute-start.2 = (bf16[1280,128]{1,0:T(8,128)(2,1)}, bf16[1280,128]{1,0:T(8,128)(2,1)S(1)}, u32[]{:S(2)}, u32[]{:S(2)}) collective-permute-start(bf16[1280,128]{1,0:T(8,128)(2,1)} %collective-permute-done), channel_id=1, source_target_pairs={{0,6},{2,4},{4,2},{6,0},{1,7},{3,5},{5,3},{7,1},{8,14},{10,12},{12... | collective-permute-start | bytes 983048 | tf_op jit(solution)/shard_map/ppermute | solution.py:17
  64.5 6.2 %collective-permute-start.3 = (bf16[1024,256]{1,0:T(8,128)(2,1)}, bf16[1024,256]{1,0:T(8,128)(2,1)}, u32[]{:S(2)}, u32[]{:S(2)}) collective-permute-start(bf16[1024,256]{1,0:T(8,128)(2,1)} %param.6), channel_id=1, source_target_pairs={{0,2},{2,0},{4,6},{6,4},{1,3},{3,1},{5,7},{7,5},{8,10},{10,8},{12,... | collective-permute-start | bytes 1572872 | tf_op jit(solution)/shard_map/ppermute | solution.py:17
  70.7 2.5 collective-permute-start.5
  74.3 2.2 fusion.35
  76.8 1.3 convolution_add_fusion
  78.2 2.0 fusion.36
  80.2 1.1 fusion.38
  81.4 11.6 %collective-permute-done.2 = bf16[1280,128]{1,0:T(8,128)(2,1)S(1)} collective-permute-done((bf16[1280,128]{1,0:T(8,128)(2,1)}, bf16[1280,128]{1,0:T(8,128)(2,1)S(1)}, u32[]{:S(2)}, u32[]{:S(2)}) %collective-permute-start.2) | collective-permute-done | bytes 327712 | tf_op jit(solution)/shard_map/ppermute | solution.py:17
  93.0 24.6 %collective-permute-done.3 = bf16[1024,256]{1,0:T(8,128)(2,1)} collective-permute-done((bf16[1024,256]{1,0:T(8,128)(2,1)}, bf16[1024,256]{1,0:T(8,128)(2,1)}, u32[]{:S(2)}, u32[]{:S(2)}) %collective-permute-start.3) | collective-permute-done | bytes 524320 | tf_op jit(solution)/shard_map/ppermute | solution.py:17
  117.6 3.0 %collective-permute-start.6 = (bf16[1024,256]{1,0:T(8,128)(2,1)}, bf16[1024,256]{1,0:T(8,128)(2,1)S(1)}, u32[]{:S(2)}, u32[]{:S(2)}) collective-permute-start(bf16[1024,256]{1,0:T(8,128)(2,1)} %collective-permute-done.3), channel_id=1, source_target_pairs={{0,1},{1,0},{2,3},{3,2},{4,5},{5,4},{6,7},{7,6},{8,9},{9,8},{10,11... | collective-permute-start | bytes 1572872 | tf_op jit(solution)/shard_map/ppermute | solution.py:17
  120.6 1.3 fusion.26
  123.5 2.3 collective-permute-start.7
  126.1 1.2 broadcast_in_dim.13
  127.3 4.5 %all-to-all-start.1 = ((bf16[4,1280,128]{1,2,0:T(8,128)(2,1)}), bf16[4,1280,128]{1,2,0:T(8,128)(2,1)S(1)}, u32[]{:S(2)}, u32[]{:S(2)}) async-start(bf16[4,1280,128]{1,2,0:T(8,128)(2,1)} %broadcast_in_dim.13), calls=%async_computation.1 | async-start | bytes 2621440 | tf_op jit(solution)/shard_map/all_to_all | solution.py:56
  132.6 2.0 convolution_bitcast_fusion
  134.6 4.8 %fusion.3 = bf16[4,512,512]{2,1,0:T(8,128)(2,1)S(1)} fusion(bf16[4,1024,512]{2,1,0:T(8,128)(2,1)} %all-to-all-done, bf16[1024,256]{1,0:T(8,128)(2,1)} %collective-permute-done.7, bf16[1024,256]{1,0:T(8,128)(2,1)} %add_convert_fusion), kind=kOutput, calls=%fused_computation.36 | convolution fusion | flops 2149580800 | bytes 7340032 | tf_op jit(solution)/shard_map/btf,tc->bfc/dot_general | solution.py:31
  139.6 9.8 %all-to-all-done.1 = bf16[4,1280,128]{1,2,0:T(8,128)(2,1)S(1)} async-done(((bf16[4,1280,128]{1,2,0:T(8,128)(2,1)}), bf16[4,1280,128]{1,2,0:T(8,128)(2,1)S(1)}, u32[]{:S(2)}, u32[]{:S(2)}) %all-to-all-start.1) | async-done | bytes 1310752 | tf_op jit(solution)/shard_map/all_to_all | solution.py:56
  149.4 1.9 convolution_convert_fusion
  151.3 1.5 pad_maximum_fusion
  154.9 1.2 fusion.39
  156.2 3.3 %collective-permute-start.8 = (bf16[1024,128]{1,0:T(8,128)(2,1)}, bf16[1024,128]{1,0:T(8,128)(2,1)}, u32[]{:S(2)}, u32[]{:S(2)}) collective-permute-start(bf16[1024,128]{1,0:T(8,128)(2,1)} %slice.89), channel_id=1, source_target_pairs={{0,1},{1,0},{2,3},{3,2},{4,5},{5,4},{6,7},{7,6},{8,9},{9,8},{10,11... | collective-permute-start | bytes 786440 | tf_op jit(solution)/shard_map/ppermute | solution.py:17
  159.5 4.5 %all-to-all-start.2 = ((bf16[4,512,512]{2,1,0:T(8,128)(2,1)}), bf16[4,512,512]{2,1,0:T(8,128)(2,1)}, u32[]{:S(2)}, u32[]{:S(2)}) async-start(bf16[4,512,512]{2,1,0:T(8,128)(2,1)} %pad_maximum_fusion), calls=%async_computation.2 | async-start | bytes 4194304 | tf_op jit(solution)/shard_map/all_to_all | solution.py:56
  164.0 1.5 convolution_bitcast_fusion.1
  166.2 1.9 collective-permute-start.12
  168.2 1.2 fusion.40
  170.6 1.9 collective-permute-start.9
  172.5 1.9 collective-permute-start.10
  174.5 5.2 %collective-permute-start.11 = (bf16[256,384]{1,0:T(8,128)(2,1)S(1)}, bf16[256,384]{1,0:T(8,128)(2,1)}, u32[]{:S(2)}, u32[]{:S(2)}) collective-permute-start(bf16[256,384]{1,0:T(8,128)(2,1)S(1)} %get-tuple-element.61), channel_id=1, source_target_pairs={{0,96},{32,0},{64,32},{96,64},{1,97},{33,1},{65,33},{97,65},{2,98}... | collective-permute-start | bytes 589832 | tf_op jit(solution)/shard_map/ppermute | solution.py:13
  181.2 3.6 %collective-permute-start.13 = (bf16[8,128,128]{1,2,0:T(8,128)(2,1)S(1)}, bf16[8,128,128]{1,2,0:T(8,128)(2,1)S(1)}, u32[]{:S(2)}, u32[]{:S(2)}) collective-permute-start(bf16[8,128,128]{1,2,0:T(8,128)(2,1)S(1)} %bitcast.123), channel_id=1, source_target_pairs={{0,128},{128,256},{256,384},{384,0},{1,129},{129,257},{257,385},{3... | collective-permute-start | bytes 786440 | tf_op jit(solution)/shard_map/ppermute | solution.py:13
  184.8 4.3 %collective-permute-start.14 = (bf16[8,128,128]{1,2,0:T(8,128)(2,1)S(1)}, bf16[8,128,128]{1,2,0:T(8,128)(2,1)S(1)}, u32[]{:S(2)}, u32[]{:S(2)}) collective-permute-start(bf16[8,128,128]{1,2,0:T(8,128)(2,1)S(1)} %bitcast.122), channel_id=1, source_target_pairs={{0,256},{128,384},{256,0},{384,128},{1,257},{129,385},{257,1},{385... | collective-permute-start | bytes 786440 | tf_op jit(solution)/shard_map/ppermute | solution.py:13
  189.1 3.1 %collective-permute-start.15 = (bf16[8,128,128]{1,2,0:T(8,128)(2,1)S(1)}, bf16[8,128,128]{1,2,0:T(8,128)(2,1)S(1)}, u32[]{:S(2)}, u32[]{:S(2)}) collective-permute-start(bf16[8,128,128]{1,2,0:T(8,128)(2,1)S(1)} %bitcast.121), channel_id=1, source_target_pairs={{0,384},{128,0},{256,128},{384,256},{1,385},{129,1},{257,129},{385... | collective-permute-start | bytes 786440 | tf_op jit(solution)/shard_map/ppermute | solution.py:13
  193.6 3.0 %collective-permute-done.13 = bf16[8,128,128]{1,2,0:T(8,128)(2,1)S(1)} collective-permute-done((bf16[8,128,128]{1,2,0:T(8,128)(2,1)S(1)}, bf16[8,128,128]{1,2,0:T(8,128)(2,1)S(1)}, u32[]{:S(2)}, u32[]{:S(2)}) %collective-permute-start.13) | collective-permute-done | bytes 262176 | tf_op jit(solution)/shard_map/ppermute | solution.py:13
  196.6 5.1 %collective-permute-done.14 = bf16[8,128,128]{1,2,0:T(8,128)(2,1)S(1)} collective-permute-done((bf16[8,128,128]{1,2,0:T(8,128)(2,1)S(1)}, bf16[8,128,128]{1,2,0:T(8,128)(2,1)S(1)}, u32[]{:S(2)}, u32[]{:S(2)}) %collective-permute-start.14) | collective-permute-done | bytes 262176 | tf_op jit(solution)/shard_map/ppermute | solution.py:13
  202.1 2.9 %collective-permute-start.16 = (bf16[8,512,128]{1,2,0:T(8,128)(2,1)S(1)}, bf16[8,512,128]{1,2,0:T(8,128)(2,1)}, u32[]{:S(2)}, u32[]{:S(2)}) collective-permute-start(bf16[8,512,128]{1,2,0:T(8,128)(2,1)S(1)} %pad_maximum_fusion.6), channel_id=1, source_target_pairs={{0,1},{1,0},{2,3},{3,2},{4,5},{5,4},{6,7},{7,6},{8,9},{9,8},{10,11... | collective-permute-start | bytes 3145736 | tf_op jit(solution)/shard_map/ppermute | solution.py:17
  206.0 3.5 %all-to-all-start.3 = ((bf16[4,256,384]{2,1,0:T(8,128)(2,1)}), bf16[4,256,384]{2,1,0:T(8,128)(2,1)S(1)}, u32[]{:S(2)}, u32[]{:S(2)}) async-start(bf16[4,256,384]{2,1,0:T(8,128)(2,1)} %broadcast_in_dim.15), calls=%async_computation.3 | async-start | bytes 1572864 | tf_op jit(solution)/shard_map/all_to_all | solution.py:56
  209.5 2.2 reduce_sum.36
  212.4 1.9 collective-permute-start.17
  214.3 2.4 fusion.10
  216.6 5.2 %all-to-all-done.3 = bf16[4,256,384]{2,1,0:T(8,128)(2,1)S(1)} async-done(((bf16[4,256,384]{2,1,0:T(8,128)(2,1)}), bf16[4,256,384]{2,1,0:T(8,128)(2,1)S(1)}, u32[]{:S(2)}, u32[]{:S(2)}) %all-to-all-start.3) | async-done | bytes 786464 | tf_op jit(solution)/shard_map/all_to_all | solution.py:56
  222.0 2.1 fusion
  224.3 33.3 %all_to_all.25 = bf16[4,256,640]{2,1,0:T(8,128)(2,1)S(1)} all-to-all(bf16[4,256,640]{2,1,0:T(8,128)(2,1)S(1)} %pad_maximum_fusion.1), channel_id=1, replica_groups=mesh['x'=4,'l'=4,'y'=4,'h'=4,'k'=2] {'l'}, dimensions={0} | all-to-all | bytes 2621440 | tf_op jit(solution)/shard_map/all_to_all | solution.py:56
  (99 shorter events, 20.0 us)
Async XLA Ops:
  0.6 1.0 copy-start
  0.6 49.0 %copy-start.1 = (bf16[1024,128]{1,0:T(8,128)(2,1)S(1)}, bf16[1024,128]{1,0:T(8,128)(2,1)}, u32[]{:S(2)}) copy-start(bf16[1024,128]{1,0:T(8,128)(2,1)} %param.5) | copy-start | bytes 786436
  2.6 41.3 %collective-permute-start.1 = (bf16[1280,128]{1,0:T(8,128)(2,1)S(1)}, bf16[1280,128]{1,0:T(8,128)(2,1)S(1)}, u32[]{:S(2)}, u32[]{:S(2)}) collective-permute-start(bf16[1280,128]{1,0:T(8,128)(2,1)S(1)} %pad_maximum_fusion.7), channel_id=1, source_target_pairs={{0,6},{2,4},{4,2},{6,0},{1,7},{3,5},{5,3},{7,1},{8,14},{10,12},{12... | collective-permute-start | bytes 983048 | tf_op jit(solution)/shard_map/ppermute | solution.py:17
  15.9 32.0 %collective-permute-start = (bf16[1280,128]{1,0:T(8,128)(2,1)S(1)}, bf16[1280,128]{1,0:T(8,128)(2,1)}, u32[]{:S(2)}, u32[]{:S(2)}) collective-permute-start(bf16[1280,128]{1,0:T(8,128)(2,1)S(1)} %pad_maximum_fusion.7), channel_id=1, source_target_pairs={{0,2},{2,0},{4,6},{6,4},{1,3},{3,1},{5,7},{7,5},{8,10},{10,8},{12,... | collective-permute-start | bytes 983048 | tf_op jit(solution)/shard_map/ppermute | solution.py:17
  52.2 5.0 %copy-start.7 = (bf16[1024,256]{1,0:T(8,128)(2,1)S(1)}, bf16[1024,256]{1,0:T(8,128)(2,1)}, u32[]{:S(2)}) copy-start(bf16[1024,256]{1,0:T(8,128)(2,1)} %param.9) | copy-start | bytes 1572868
  52.2 65.5 %all-to-all-start = ((bf16[4,1024,512]{2,1,0:T(8,128)(2,1)}), bf16[4,1024,512]{2,1,0:T(8,128)(2,1)}, u32[]{:S(2)}, u32[]{:S(2)}) async-start(bf16[4,1024,512]{2,1,0:T(8,128)(2,1)} %broadcast_in_dim.12), calls=%async_computation | async-start | bytes 8388608 | tf_op jit(solution)/shard_map/all_to_all | solution.py:56
  57.3 19.2 %collective-permute-start.4 = (bf16[1024,256]{1,0:T(8,128)(2,1)}, bf16[1024,256]{1,0:T(8,128)(2,1)S(1)}, u32[]{:S(2)}, u32[]{:S(2)}) collective-permute-start(bf16[1024,256]{1,0:T(8,128)(2,1)} %param.6), channel_id=1, source_target_pairs={{0,1},{1,0},{2,3},{3,2},{4,5},{5,4},{6,7},{7,6},{8,9},{9,8},{10,11... | collective-permute-start | bytes 1572872 | tf_op jit(solution)/shard_map/ppermute | solution.py:17
  60.3 32.7 %collective-permute-start.2 = (bf16[1280,128]{1,0:T(8,128)(2,1)}, bf16[1280,128]{1,0:T(8,128)(2,1)S(1)}, u32[]{:S(2)}, u32[]{:S(2)}) collective-permute-start(bf16[1280,128]{1,0:T(8,128)(2,1)} %collective-permute-done), channel_id=1, source_target_pairs={{0,6},{2,4},{4,2},{6,0},{1,7},{3,5},{5,3},{7,1},{8,14},{10,12},{12... | collective-permute-start | bytes 983048 | tf_op jit(solution)/shard_map/ppermute | solution.py:17
  64.5 53.1 %collective-permute-start.3 = (bf16[1024,256]{1,0:T(8,128)(2,1)}, bf16[1024,256]{1,0:T(8,128)(2,1)}, u32[]{:S(2)}, u32[]{:S(2)}) collective-permute-start(bf16[1024,256]{1,0:T(8,128)(2,1)} %param.6), channel_id=1, source_target_pairs={{0,2},{2,0},{4,6},{6,4},{1,3},{3,1},{5,7},{7,5},{8,10},{10,8},{12,... | collective-permute-start | bytes 1572872 | tf_op jit(solution)/shard_map/ppermute | solution.py:17
  70.7 9.5 %collective-permute-start.5 = (bf16[1024,512]{1,0:T(8,128)(2,1)S(1)}, bf16[1024,512]{1,0:T(8,128)(2,1)S(1)}, u32[]{:S(2)}, u32[]{:S(2)}) collective-permute-start(bf16[1024,512]{1,0:T(8,128)(2,1)S(1)} %maximum_maximum_fusion), channel_id=1, source_target_pairs={{0,1},{1,0},{2,3},{3,2},{4,5},{5,4},{6,7},{7,6},{8,9},{9,8},{10,11... | collective-permute-start | bytes 3145736 | tf_op jit(solution)/shard_map/ppermute | solution.py:17
  93.0 32.8 %copy-start.2 = (bf16[1280,128]{1,0:T(8,128)(2,1)}, bf16[1280,128]{1,0:T(8,128)(2,1)S(1)}, u32[]{:S(2)}) copy-start(bf16[1280,128]{1,0:T(8,128)(2,1)S(1)} %collective-permute-done.2) | copy-start | bytes 983044
  117.6 4.7 %collective-permute-start.6 = (bf16[1024,256]{1,0:T(8,128)(2,1)}, bf16[1024,256]{1,0:T(8,128)(2,1)S(1)}, u32[]{:S(2)}, u32[]{:S(2)}) collective-permute-start(bf16[1024,256]{1,0:T(8,128)(2,1)} %collective-permute-done.3), channel_id=1, source_target_pairs={{0,1},{1,0},{2,3},{3,2},{4,5},{5,4},{6,7},{7,6},{8,9},{9,8},{10,11... | collective-permute-start | bytes 1572872 | tf_op jit(solution)/shard_map/ppermute | solution.py:17
  122.4 1.1 copy-start.5
  123.5 11.2 %collective-permute-start.7 = (bf16[1024,256]{1,0:T(8,128)(2,1)}, bf16[1024,256]{1,0:T(8,128)(2,1)}, u32[]{:S(2)}, u32[]{:S(2)}) collective-permute-start(bf16[1024,256]{1,0:T(8,128)(2,1)} %add_convert_fusion), channel_id=1, source_target_pairs={{0,1},{1,0},{2,3},{3,2},{4,5},{5,4},{6,7},{7,6},{8,9},{9,8},{10,11... | collective-permute-start | bytes 1572872 | tf_op jit(solution)/shard_map/ppermute | solution.py:17
  126.0 5.8 %copy-start.11 = (s32[32]{0:T(128)S(1)}, s32[32]{0:T(128)}, u32[]{:S(2)}) copy-start(s32[32]{0:T(128)} %param.8) | copy-start | bytes 388
  126.1 5.8 %copy-start.3 = (bf16[1280,128]{1,0:T(8,128)(2,1)S(1)}, bf16[1280,128]{1,0:T(8,128)(2,1)}, u32[]{:S(2)}) copy-start(bf16[1280,128]{1,0:T(8,128)(2,1)} %copy-done.2) | copy-start | bytes 983044
  127.3 5.3 %copy-start.6 = (bf16[1024,256]{1,0:T(8,128)(2,1)S(1)}, bf16[1024,256]{1,0:T(8,128)(2,1)}, u32[]{:S(2)}) copy-start(bf16[1024,256]{1,0:T(8,128)(2,1)} %copy-done.5) | copy-start | bytes 1572868
  127.3 22.1 %all-to-all-start.1 = ((bf16[4,1280,128]{1,2,0:T(8,128)(2,1)}), bf16[4,1280,128]{1,2,0:T(8,128)(2,1)S(1)}, u32[]{:S(2)}, u32[]{:S(2)}) async-start(bf16[4,1280,128]{1,2,0:T(8,128)(2,1)} %broadcast_in_dim.13), calls=%async_computation.1 | async-start | bytes 2621440 | tf_op jit(solution)/shard_map/all_to_all | solution.py:56
  156.2 9.4 %copy-start.8 = (bf16[256,256]{1,0:T(8,128)(2,1)S(1)}, bf16[256,256]{1,0:T(8,128)(2,1)}, u32[]{:S(2)}) copy-start(bf16[256,256]{1,0:T(8,128)(2,1)} %fusion.35) | copy-start | bytes 393220
  156.2 9.4 %copy-start.9 = (bf16[256,256]{1,0:T(8,128)(2,1)S(1)}, bf16[256,256]{1,0:T(8,128)(2,1)}, u32[]{:S(2)}) copy-start(bf16[256,256]{1,0:T(8,128)(2,1)} %fusion.36) | copy-start | bytes 393220
  156.2 9.4 %copy-start.10 = (bf16[1,256,256]{2,1,0:T(8,128)(2,1)S(1)}, bf16[1,256,256]{2,1,0:T(8,128)(2,1)}, u32[]{:S(2)}) copy-start(bf16[1,256,256]{2,1,0:T(8,128)(2,1)} %convolution_bitcast_fusion) | copy-start | bytes 393220
  156.2 12.0 %collective-permute-start.8 = (bf16[1024,128]{1,0:T(8,128)(2,1)}, bf16[1024,128]{1,0:T(8,128)(2,1)}, u32[]{:S(2)}, u32[]{:S(2)}) collective-permute-start(bf16[1024,128]{1,0:T(8,128)(2,1)} %slice.89), channel_id=1, source_target_pairs={{0,1},{1,0},{2,3},{3,2},{4,5},{5,4},{6,7},{7,6},{8,9},{9,8},{10,11... | collective-permute-start | bytes 786440 | tf_op jit(solution)/shard_map/ppermute | solution.py:17
  159.5 42.2 %all-to-all-start.2 = ((bf16[4,512,512]{2,1,0:T(8,128)(2,1)}), bf16[4,512,512]{2,1,0:T(8,128)(2,1)}, u32[]{:S(2)}, u32[]{:S(2)}) async-start(bf16[4,512,512]{2,1,0:T(8,128)(2,1)} %pad_maximum_fusion), calls=%async_computation.2 | async-start | bytes 4194304 | tf_op jit(solution)/shard_map/all_to_all | solution.py:56
  166.0 2.1 slice-start
  166.0 3.4 %slice-start.1 = ((bf16[512,128]{1,0:T(8,128)(2,1)}), bf16[384,128]{1,0:T(8,128)(2,1)S(1)}, s32[]{:S(2)}) async-start(bf16[512,128]{1,0:T(8,128)(2,1)} %fusion.38), calls=%async_computation.6 | async-start | bytes 196608 | tf_op jit(solution)/shard_map/slice | solution.py:115
  166.2 13.5 %collective-permute-start.12 = (bf16[16,128,128]{2,1,0:T(8,128)(2,1)S(1)}, bf16[16,128,128]{2,1,0:T(8,128)(2,1)S(1)}, u32[]{:S(2)}, u32[]{:S(2)}) collective-permute-start(bf16[16,128,128]{2,1,0:T(8,128)(2,1)S(1)} %get-tuple-element.58), channel_id=1, source_target_pairs={{0,1},{1,0},{2,3},{3,2},{4,5},{5,4},{6,7},{7,6},{8,9},{9,8},{10,11... | collective-permute-start | bytes 1572872 | tf_op jit(solution)/shard_map/ppermute | solution.py:17
  170.6 18.5 %collective-permute-start.9 = (bf16[256,384]{1,0:T(8,128)(2,1)}, bf16[256,384]{1,0:T(8,128)(2,1)S(1)}, u32[]{:S(2)}, u32[]{:S(2)}) collective-permute-start(bf16[256,384]{1,0:T(8,128)(2,1)} %get-tuple-element.59), channel_id=1, source_target_pairs={{0,32},{32,64},{64,96},{96,0},{1,33},{33,65},{65,97},{97,1},{2,34}... | collective-permute-start | bytes 589832 | tf_op jit(solution)/shard_map/ppermute | solution.py:13
  172.5 19.8 %collective-permute-start.10 = (bf16[256,384]{1,0:T(8,128)(2,1)}, bf16[256,384]{1,0:T(8,128)(2,1)}, u32[]{:S(2)}, u32[]{:S(2)}) collective-permute-start(bf16[256,384]{1,0:T(8,128)(2,1)} %get-tuple-element.60), channel_id=1, source_target_pairs={{0,64},{32,96},{64,0},{96,32},{1,65},{33,97},{65,1},{97,33},{2,66}... | collective-permute-start | bytes 589832 | tf_op jit(solution)/shard_map/ppermute | solution.py:13
  174.5 17.9 %collective-permute-start.11 = (bf16[256,384]{1,0:T(8,128)(2,1)S(1)}, bf16[256,384]{1,0:T(8,128)(2,1)}, u32[]{:S(2)}, u32[]{:S(2)}) collective-permute-start(bf16[256,384]{1,0:T(8,128)(2,1)S(1)} %get-tuple-element.61), channel_id=1, source_target_pairs={{0,96},{32,0},{64,32},{96,64},{1,97},{33,1},{65,33},{97,65},{2,98}... | collective-permute-start | bytes 589832 | tf_op jit(solution)/shard_map/ppermute | solution.py:13
  181.2 15.4 %collective-permute-start.13 = (bf16[8,128,128]{1,2,0:T(8,128)(2,1)S(1)}, bf16[8,128,128]{1,2,0:T(8,128)(2,1)S(1)}, u32[]{:S(2)}, u32[]{:S(2)}) collective-permute-start(bf16[8,128,128]{1,2,0:T(8,128)(2,1)S(1)} %bitcast.123), channel_id=1, source_target_pairs={{0,128},{128,256},{256,384},{384,0},{1,129},{129,257},{257,385},{3... | collective-permute-start | bytes 786440 | tf_op jit(solution)/shard_map/ppermute | solution.py:13
  184.8 16.9 %collective-permute-start.14 = (bf16[8,128,128]{1,2,0:T(8,128)(2,1)S(1)}, bf16[8,128,128]{1,2,0:T(8,128)(2,1)S(1)}, u32[]{:S(2)}, u32[]{:S(2)}) collective-permute-start(bf16[8,128,128]{1,2,0:T(8,128)(2,1)S(1)} %bitcast.122), channel_id=1, source_target_pairs={{0,256},{128,384},{256,0},{384,128},{1,257},{129,385},{257,1},{385... | collective-permute-start | bytes 786440 | tf_op jit(solution)/shard_map/ppermute | solution.py:13
  189.1 12.6 %collective-permute-start.15 = (bf16[8,128,128]{1,2,0:T(8,128)(2,1)S(1)}, bf16[8,128,128]{1,2,0:T(8,128)(2,1)S(1)}, u32[]{:S(2)}, u32[]{:S(2)}) collective-permute-start(bf16[8,128,128]{1,2,0:T(8,128)(2,1)S(1)} %bitcast.121), channel_id=1, source_target_pairs={{0,384},{128,0},{256,128},{384,256},{1,385},{129,1},{257,129},{385... | collective-permute-start | bytes 786440 | tf_op jit(solution)/shard_map/ppermute | solution.py:13
  202.0 3.0 %copy-start.4 = (bf16[8,128,128]{1,2,0:T(8,128)(2,1)}, bf16[8,128,128]{1,2,0:T(8,128)(2,1)S(1)}, u32[]{:S(2)}) copy-start(bf16[8,128,128]{1,2,0:T(8,128)(2,1)S(1)} %get-tuple-element.52) | copy-start | bytes 786436
  202.1 19.9 %collective-permute-start.16 = (bf16[8,512,128]{1,2,0:T(8,128)(2,1)S(1)}, bf16[8,512,128]{1,2,0:T(8,128)(2,1)}, u32[]{:S(2)}, u32[]{:S(2)}) collective-permute-start(bf16[8,512,128]{1,2,0:T(8,128)(2,1)S(1)} %pad_maximum_fusion.6), channel_id=1, source_target_pairs={{0,1},{1,0},{2,3},{3,2},{4,5},{5,4},{6,7},{7,6},{8,9},{9,8},{10,11... | collective-permute-start | bytes 3145736 | tf_op jit(solution)/shard_map/ppermute | solution.py:17
  206.0 15.9 %all-to-all-start.3 = ((bf16[4,256,384]{2,1,0:T(8,128)(2,1)}), bf16[4,256,384]{2,1,0:T(8,128)(2,1)S(1)}, u32[]{:S(2)}, u32[]{:S(2)}) async-start(bf16[4,256,384]{2,1,0:T(8,128)(2,1)} %broadcast_in_dim.15), calls=%async_computation.3 | async-start | bytes 1572864 | tf_op jit(solution)/shard_map/all_to_all | solution.py:56
  212.4 9.7 %collective-permute-start.17 = (bf16[512,256]{1,0:T(8,128)(2,1)}, bf16[512,256]{1,0:T(8,128)(2,1)}, u32[]{:S(2)}, u32[]{:S(2)}) collective-permute-start(bf16[512,256]{1,0:T(8,128)(2,1)} %slice.115), channel_id=1, source_target_pairs={{0,1},{1,0},{2,3},{3,2},{4,5},{5,4},{6,7},{7,6},{8,9},{9,8},{10,11... | collective-permute-start | bytes 786440 | tf_op jit(solution)/shard_map/ppermute | solution.py:17

commit v3 on v2

--- a/solution.py
+++ b/solution.py
@@ -134,7 +134,6 @@
     side = jnp.concatenate([side[:, : 2 * held], third[:, tokens:], side[:, 3 * held :]], 1)
     ordered = block_panels(side, panel_slot, h, k)
     rows_got = [pick(ordered, x)] + [shifted(pick(ordered, (x + s) % 4), "x", s) for s in SHIFTS]
-    got, quarter, *rows_got = together(got, quarter, *rows_got)
     rows_got = jnp.stack(rows_got)
     left = jnp.concatenate([pick(rows_got, (x - (h ^ m)) % 4) for m in (0, 1, 3, 2)], 1)
     left_other = swapped(left, "k", 1)

time: 262 us -> 278 us (1.061)
  local copies, waits for them, and re-layouts: 14.4 us -> 25.6 us
  waiting for transfers between devices: 86.6 us -> 76.9 us
  starting transfers between devices: 86.9 us -> 94.3 us
  other arithmetic: 9.9 us -> 14.1 us
  blocking collectives: 33.3 us -> 36.4 us
    ppermute x12, starting transfers between devices: 49.5 us -> 60.1 us  [swapped(): lax.ppermute(value, axis, [(i, i ^ mask) for i in range(lax.axis_size(axi...]
    dynamic_slice x5 -> x4, local copies, waits for them, and re-layouts: 0.84 us -> 7.46 us  [pick(): return lax.dynamic_index_in_dim(stacked, index, 0, keepdims=False)]
    ppermute x12, waiting for transfers between devices: 63.4 us -> 57.2 us  [swapped(): lax.ppermute(value, axis, [(i, i ^ mask) for i in range(lax.axis_size(axi...]
    all_to_all x1, blocking collectives: 33.3 us -> 36.4 us  [exchanged(): return lax.all_to_all(pieces, axes, 0, 0, tiled=True)]
    ppermute x6, starting transfers between devices: 20 us -> 17 us  [shifted(): lax.ppermute(value, axis, [(i, (i + shift) % size) for i in range(size)])]
  transfers between devices with their start and end apart: 22 -> 22, of which waited for: 9 -> 9; matrix products, arithmetic and copies ran while one was open for 12% -> 18% of each run, Pallas kernels for 0% -> 0%
where the time goes in v3:
time: 278 us; the launch traced here: 276 us
  starting transfers between devices  94.3 us (34%)
  waiting for transfers between devices  76.9 us (28%)
  blocking collectives  36.4 us (13%)
  matrix products  27.1 us (10%)
  local copies, waits for them, and re-layouts  25.6 us (9%)
  other arithmetic  14.1 us (5%)
    ppermute x12, starting transfers between devices, swapped(): lax.ppermute(value, axis, [(i, i ^ mask) for i in range(lax.axis_size(axi...  60.1 us
    ppermute x12, waiting for transfers between devices, swapped(): lax.ppermute(value, axis, [(i, i ^ mask) for i in range(lax.axis_size(axi...  57.2 us
    all_to_all x1, blocking collectives, exchanged(): return lax.all_to_all(pieces, axes, 0, 0, tiled=True)  36.4 us
    all_to_all x4, starting transfers between devices, exchanged(): return lax.all_to_all(pieces, axes, 0, 0, tiled=True)  17.2 us
    ppermute x6, starting transfers between devices, shifted(): lax.ppermute(value, axis, [(i, (i + shift) % size) for i in range(size)])  17 us
    all_to_all x4, waiting for transfers between devices, exchanged(): return lax.all_to_all(pieces, axes, 0, 0, tiled=True)  14 us
    dot_general x8, matrix products, contract_rows(): lax.dot_general(first_operand, second_operand, (((0,), (0,)), ((), ())),...  12.6 us
    dot_general x4, matrix products, contract_tokens(): jnp.einsum('btf,tc->bfc', stacked, values, preferred_element_type=jnp.flo...  10.5 us
  transfers between devices with their start and end apart: 22, of which 9 were waited for; matrix products, arithmetic and copies ran while one was open for 18% of the time, Pallas kernels for 0%

profile of v3, /device:TPU:1, one launch (start us, length us, event | category | flops | bytes accessed | tf_op | source)
XLA Modules:
  0.0 275.9 jit_solution(2165444597608244416)
XLA Ops:
  2.6 9.6 %collective-permute-start = (bf16[1280,128]{1,0:T(8,128)(2,1)S(1)}, bf16[1280,128]{1,0:T(8,128)(2,1)}, u32[]{:S(2)}, u32[]{:S(2)}) collective-permute-start(bf16[1280,128]{1,0:T(8,128)(2,1)S(1)} %pad_maximum_fusion.7), channel_id=1, source_target_pairs={{0,2},{2,0},{4,6},{6,4},{1,3},{3,1},{5,7},{7,5},{8,10},{10,8},{12,... | collective-permute-start | bytes 983048 | tf_op jit(solution)/shard_map/ppermute | solution.py:17
  12.2 8.8 %collective-permute-start.1 = (bf16[1280,128]{1,0:T(8,128)(2,1)S(1)}, bf16[1280,128]{1,0:T(8,128)(2,1)S(1)}, u32[]{:S(2)}, u32[]{:S(2)}) collective-permute-start(bf16[1280,128]{1,0:T(8,128)(2,1)S(1)} %pad_maximum_fusion.7), channel_id=1, source_target_pairs={{0,6},{2,4},{4,2},{6,0},{1,7},{3,5},{5,3},{7,1},{8,14},{10,12},{12... | collective-permute-start | bytes 983048 | tf_op jit(solution)/shard_map/ppermute | solution.py:17
  21.0 19.2 %collective-permute-done = bf16[1280,128]{1,0:T(8,128)(2,1)} collective-permute-done((bf16[1280,128]{1,0:T(8,128)(2,1)S(1)}, bf16[1280,128]{1,0:T(8,128)(2,1)}, u32[]{:S(2)}, u32[]{:S(2)}) %collective-permute-start) | collective-permute-done | bytes 327712 | tf_op jit(solution)/shard_map/ppermute | solution.py:17
  43.1 2.4 broadcast_in_dim.12
  45.4 5.0 %all-to-all-start = ((bf16[4,1024,512]{2,1,0:T(8,128)(2,1)}), bf16[4,1024,512]{2,1,0:T(8,128)(2,1)}, u32[]{:S(2)}, u32[]{:S(2)}) async-start(bf16[4,1024,512]{2,1,0:T(8,128)(2,1)} %broadcast_in_dim.12), calls=%async_computation | async-start | bytes 8388608 | tf_op jit(solution)/shard_map/all_to_all | solution.py:56
  50.6 11.0 %collective-permute-start.4 = (bf16[1024,256]{1,0:T(8,128)(2,1)}, bf16[1024,256]{1,0:T(8,128)(2,1)S(1)}, u32[]{:S(2)}, u32[]{:S(2)}) collective-permute-start(bf16[1024,256]{1,0:T(8,128)(2,1)} %param.6), channel_id=1, source_target_pairs={{0,1},{1,0},{2,3},{3,2},{4,5},{5,4},{6,7},{7,6},{8,9},{9,8},{10,11... | collective-permute-start | bytes 1572872 | tf_op jit(solution)/shard_map/ppermute | solution.py:17
  61.7 8.0 %collective-permute-start.2 = (bf16[1280,128]{1,0:T(8,128)(2,1)}, bf16[1280,128]{1,0:T(8,128)(2,1)S(1)}, u32[]{:S(2)}, u32[]{:S(2)}) collective-permute-start(bf16[1280,128]{1,0:T(8,128)(2,1)} %collective-permute-done), channel_id=1, source_target_pairs={{0,6},{2,4},{4,2},{6,0},{1,7},{3,5},{5,3},{7,1},{8,14},{10,12},{12... | collective-permute-start | bytes 983048 | tf_op jit(solution)/shard_map/ppermute | solution.py:17
  69.6 3.7 %collective-permute-start.3 = (bf16[1024,256]{1,0:T(8,128)(2,1)}, bf16[1024,256]{1,0:T(8,128)(2,1)}, u32[]{:S(2)}, u32[]{:S(2)}) collective-permute-start(bf16[1024,256]{1,0:T(8,128)(2,1)} %param.6), channel_id=1, source_target_pairs={{0,2},{2,0},{4,6},{6,4},{1,3},{3,1},{5,7},{7,5},{8,10},{10,8},{12,... | collective-permute-start | bytes 1572872 | tf_op jit(solution)/shard_map/ppermute | solution.py:17
  73.4 2.5 collective-permute-start.5
  77.0 2.2 fusion.35
  79.5 1.3 convolution_add_fusion
  80.9 2.1 fusion.36
  84.1 12.0 %collective-permute-done.2 = bf16[1280,128]{1,0:T(8,128)(2,1)S(1)} collective-permute-done((bf16[1280,128]{1,0:T(8,128)(2,1)}, bf16[1280,128]{1,0:T(8,128)(2,1)S(1)}, u32[]{:S(2)}, u32[]{:S(2)}) %collective-permute-start.2) | collective-permute-done | bytes 327712 | tf_op jit(solution)/shard_map/ppermute | solution.py:17
  96.1 24.8 %collective-permute-done.3 = bf16[1024,256]{1,0:T(8,128)(2,1)} collective-permute-done((bf16[1024,256]{1,0:T(8,128)(2,1)}, bf16[1024,256]{1,0:T(8,128)(2,1)}, u32[]{:S(2)}, u32[]{:S(2)}) %collective-permute-start.3) | collective-permute-done | bytes 524320 | tf_op jit(solution)/shard_map/ppermute | solution.py:17
  120.8 2.4 collective-permute-start.6
  123.2 1.3 fusion.26
  126.0 2.3 collective-permute-start.7
  129.9 4.5 %all-to-all-start.1 = ((bf16[4,1280,128]{1,2,0:T(8,128)(2,1)}), bf16[4,1280,128]{1,2,0:T(8,128)(2,1)S(1)}, u32[]{:S(2)}, u32[]{:S(2)}) async-start(bf16[4,1280,128]{1,2,0:T(8,128)(2,1)} %broadcast_in_dim.13), calls=%async_computation.1 | async-start | bytes 2621440 | tf_op jit(solution)/shard_map/all_to_all | solution.py:56
  135.2 2.0 convolution_bitcast_fusion
  137.3 4.8 %fusion.3 = bf16[4,512,512]{2,1,0:T(8,128)(2,1)S(1)} fusion(bf16[4,1024,512]{2,1,0:T(8,128)(2,1)} %all-to-all-done, bf16[1024,256]{1,0:T(8,128)(2,1)} %collective-permute-done.7, bf16[1024,256]{1,0:T(8,128)(2,1)} %add_convert_fusion), kind=kOutput, calls=%fused_computation.36 | convolution fusion | flops 2149580800 | bytes 7340032 | tf_op jit(solution)/shard_map/btf,tc->bfc/dot_general | solution.py:31
  142.2 9.8 %all-to-all-done.1 = bf16[4,1280,128]{1,2,0:T(8,128)(2,1)S(1)} async-done(((bf16[4,1280,128]{1,2,0:T(8,128)(2,1)}), bf16[4,1280,128]{1,2,0:T(8,128)(2,1)S(1)}, u32[]{:S(2)}, u32[]{:S(2)}) %all-to-all-start.1) | async-done | bytes 1310752 | tf_op jit(solution)/shard_map/all_to_all | solution.py:56
  152.0 2.4 convolution_convert_fusion
  154.4 1.5 pad_maximum_fusion
  156.0 3.3 %collective-permute-start.14 = (bf16[1024,128]{1,0:T(8,128)(2,1)}, bf16[1024,128]{1,0:T(8,128)(2,1)}, u32[]{:S(2)}, u32[]{:S(2)}) collective-permute-start(bf16[1024,128]{1,0:T(8,128)(2,1)} %slice.89), channel_id=1, source_target_pairs={{0,1},{1,0},{2,3},{3,2},{4,5},{5,4},{6,7},{7,6},{8,9},{9,8},{10,11... | collective-permute-start | bytes 786440 | tf_op jit(solution)/shard_map/ppermute | solution.py:17
  160.5 1.7 slice.92
  163.3 1.5 convolution_bitcast_fusion.1
  165.9 4.1 %all-to-all-start.2 = ((bf16[4,512,512]{2,1,0:T(8,128)(2,1)}), bf16[4,512,512]{2,1,0:T(8,128)(2,1)S(1)}, u32[]{:S(2)}, u32[]{:S(2)}) async-start(bf16[4,512,512]{2,1,0:T(8,128)(2,1)} %pad_maximum_fusion), calls=%async_computation.2 | async-start | bytes 4194304 | tf_op jit(solution)/shard_map/all_to_all | solution.py:56
  172.1 2.2 collective-permute-start.8
  177.0 2.9 %gather_fusion = bf16[32,128,128]{2,1,0:T(8,128)(2,1)} fusion(bf16[32,128,128]{2,1,0:T(8,128)(2,1)} %pad_maximum_fusion.3, s32[1024]{0:T(1024)S(1)} %pad_clamp_fusion), kind=kCustom, calls=%fused_computation | custom fusion | bytes 2097280 | tf_op jit(solution)/shard_map/jit(_take)/gather | solution.py:70
  179.9 2.1 constant_dynamic-slice_fusion.3
  182.0 1.8 copy.35
  183.8 4.9 %collective-permute-start.11 = (bf16[8,128,128]{1,2,0:T(8,128)(2,1)}, bf16[8,128,128]{1,2,0:T(8,128)(2,1)}, u32[]{:S(2)}, u32[]{:S(2)}) collective-permute-start(bf16[8,128,128]{1,2,0:T(8,128)(2,1)} %bitcast.121), channel_id=1, source_target_pairs={{0,384},{128,0},{256,128},{384,256},{1,385},{129,1},{257,129},{385... | collective-permute-start | bytes 786440 | tf_op jit(solution)/shard_map/ppermute | solution.py:13
  188.6 1.8 copy.34
  190.4 2.5 collective-permute-start.10
  192.9 1.8 copy.33
  194.7 2.5 collective-permute-start.9
  198.1 1.9 collective-permute-start.17
  200.0 1.9 collective-permute-start.16
  202.8 3.4 %collective-permute-start.15 = (bf16[256,384]{1,0:T(8,128)(2,1)}, bf16[256,384]{1,0:T(8,128)(2,1)S(1)}, u32[]{:S(2)}, u32[]{:S(2)}) collective-permute-start(bf16[256,384]{1,0:T(8,128)(2,1)} %get-tuple-element.47), channel_id=1, source_target_pairs={{0,32},{32,64},{64,96},{96,0},{1,33},{33,65},{65,97},{97,1},{2,34}... | collective-permute-start | bytes 589832 | tf_op jit(solution)/shard_map/ppermute | solution.py:13
  206.2 1.8 collective-permute-done.9
  210.8 2.7 collective-permute-start.12
  213.4 3.8 %collective-permute-done.16 = bf16[256,384]{1,0:T(8,128)(2,1)} collective-permute-done((bf16[256,384]{1,0:T(8,128)(2,1)}, bf16[256,384]{1,0:T(8,128)(2,1)}, u32[]{:S(2)}, u32[]{:S(2)}) %collective-permute-start.16) | collective-permute-done | bytes 196640 | tf_op jit(solution)/shard_map/ppermute | solution.py:13
  219.4 3.5 %all-to-all-start.3 = ((bf16[4,256,384]{2,1,0:T(8,128)(2,1)}), bf16[4,256,384]{2,1,0:T(8,128)(2,1)S(1)}, u32[]{:S(2)}, u32[]{:S(2)}) async-start(bf16[4,256,384]{2,1,0:T(8,128)(2,1)} %broadcast_in_dim.15), calls=%async_computation.3 | async-start | bytes 1572864 | tf_op jit(solution)/shard_map/all_to_all | solution.py:56
  225.1 3.7 %collective-permute-start.13 = (bf16[512,256]{1,0:T(8,128)(2,1)S(1)}, bf16[512,256]{1,0:T(8,128)(2,1)S(1)}, u32[]{:S(2)}, u32[]{:S(2)}) collective-permute-start(bf16[512,256]{1,0:T(8,128)(2,1)S(1)} %slice.111), channel_id=1, source_target_pairs={{0,1},{1,0},{2,3},{3,2},{4,5},{5,4},{6,7},{7,6},{8,9},{9,8},{10,11... | collective-permute-start | bytes 786440 | tf_op jit(solution)/shard_map/ppermute | solution.py:17
  228.8 4.2 %all-to-all-done.3 = bf16[4,256,384]{2,1,0:T(8,128)(2,1)S(1)} async-done(((bf16[4,256,384]{2,1,0:T(8,128)(2,1)}), bf16[4,256,384]{2,1,0:T(8,128)(2,1)S(1)}, u32[]{:S(2)}, u32[]{:S(2)}) %all-to-all-start.3) | async-done | bytes 786464 | tf_op jit(solution)/shard_map/all_to_all | solution.py:56
  233.2 1.6 fusion.10
  234.8 1.7 fusion
  236.7 36.4 %all_to_all.25 = bf16[4,256,640]{2,1,0:T(8,128)(2,1)S(1)} all-to-all(bf16[4,256,640]{2,1,0:T(8,128)(2,1)S(1)} %pad_maximum_fusion.1), channel_id=1, replica_groups=mesh['x'=4,'l'=4,'y'=4,'h'=4,'k'=2] {'l'}, dimensions={0} | all-to-all | bytes 2621440 | tf_op jit(solution)/shard_map/all_to_all | solution.py:56
  (112 shorter events, 31.1 us)
Async XLA Ops:
  0.6 1.0 copy-start
  0.6 42.3 %copy-start.1 = (bf16[1024,128]{1,0:T(8,128)(2,1)S(1)}, bf16[1024,128]{1,0:T(8,128)(2,1)}, u32[]{:S(2)}) copy-start(bf16[1024,128]{1,0:T(8,128)(2,1)} %param.5) | copy-start | bytes 786436
  2.6 37.7 %collective-permute-start = (bf16[1280,128]{1,0:T(8,128)(2,1)S(1)}, bf16[1280,128]{1,0:T(8,128)(2,1)}, u32[]{:S(2)}, u32[]{:S(2)}) collective-permute-start(bf16[1280,128]{1,0:T(8,128)(2,1)S(1)} %pad_maximum_fusion.7), channel_id=1, source_target_pairs={{0,2},{2,0},{4,6},{6,4},{1,3},{3,1},{5,7},{7,5},{8,10},{10,8},{12,... | collective-permute-start | bytes 983048 | tf_op jit(solution)/shard_map/ppermute | solution.py:17
  12.2 28.9 %collective-permute-start.1 = (bf16[1280,128]{1,0:T(8,128)(2,1)S(1)}, bf16[1280,128]{1,0:T(8,128)(2,1)S(1)}, u32[]{:S(2)}, u32[]{:S(2)}) collective-permute-start(bf16[1280,128]{1,0:T(8,128)(2,1)S(1)} %pad_maximum_fusion.7), channel_id=1, source_target_pairs={{0,6},{2,4},{4,2},{6,0},{1,7},{3,5},{5,3},{7,1},{8,14},{10,12},{12... | collective-permute-start | bytes 983048 | tf_op jit(solution)/shard_map/ppermute | solution.py:17
  45.4 5.1 %copy-start.13 = (bf16[1024,256]{1,0:T(8,128)(2,1)S(1)}, bf16[1024,256]{1,0:T(8,128)(2,1)}, u32[]{:S(2)}) copy-start(bf16[1024,256]{1,0:T(8,128)(2,1)} %param.9) | copy-start | bytes 1572868
  45.4 75.4 %all-to-all-start = ((bf16[4,1024,512]{2,1,0:T(8,128)(2,1)}), bf16[4,1024,512]{2,1,0:T(8,128)(2,1)}, u32[]{:S(2)}, u32[]{:S(2)}) async-start(bf16[4,1024,512]{2,1,0:T(8,128)(2,1)} %broadcast_in_dim.12), calls=%async_computation | async-start | bytes 8388608 | tf_op jit(solution)/shard_map/all_to_all | solution.py:56
  50.6 28.6 %collective-permute-start.4 = (bf16[1024,256]{1,0:T(8,128)(2,1)}, bf16[1024,256]{1,0:T(8,128)(2,1)S(1)}, u32[]{:S(2)}, u32[]{:S(2)}) collective-permute-start(bf16[1024,256]{1,0:T(8,128)(2,1)} %param.6), channel_id=1, source_target_pairs={{0,1},{1,0},{2,3},{3,2},{4,5},{5,4},{6,7},{7,6},{8,9},{9,8},{10,11... | collective-permute-start | bytes 1572872 | tf_op jit(solution)/shard_map/ppermute | solution.py:17
  61.7 34.4 %collective-permute-start.2 = (bf16[1280,128]{1,0:T(8,128)(2,1)}, bf16[1280,128]{1,0:T(8,128)(2,1)S(1)}, u32[]{:S(2)}, u32[]{:S(2)}) collective-permute-start(bf16[1280,128]{1,0:T(8,128)(2,1)} %collective-permute-done), channel_id=1, source_target_pairs={{0,6},{2,4},{4,2},{6,0},{1,7},{3,5},{5,3},{7,1},{8,14},{10,12},{12... | collective-permute-start | bytes 983048 | tf_op jit(solution)/shard_map/ppermute | solution.py:17
  69.6 51.2 %collective-permute-start.3 = (bf16[1024,256]{1,0:T(8,128)(2,1)}, bf16[1024,256]{1,0:T(8,128)(2,1)}, u32[]{:S(2)}, u32[]{:S(2)}) collective-permute-start(bf16[1024,256]{1,0:T(8,128)(2,1)} %param.6), channel_id=1, source_target_pairs={{0,2},{2,0},{4,6},{6,4},{1,3},{3,1},{5,7},{7,5},{8,10},{10,8},{12,... | collective-permute-start | bytes 1572872 | tf_op jit(solution)/shard_map/ppermute | solution.py:17
  73.4 9.5 %collective-permute-start.5 = (bf16[1024,512]{1,0:T(8,128)(2,1)S(1)}, bf16[1024,512]{1,0:T(8,128)(2,1)S(1)}, u32[]{:S(2)}, u32[]{:S(2)}) collective-permute-start(bf16[1024,512]{1,0:T(8,128)(2,1)S(1)} %maximum_maximum_fusion), channel_id=1, source_target_pairs={{0,1},{1,0},{2,3},{3,2},{4,5},{5,4},{6,7},{7,6},{8,9},{9,8},{10,11... | collective-permute-start | bytes 3145736 | tf_op jit(solution)/shard_map/ppermute | solution.py:17
  96.1 32.4 %copy-start.4 = (bf16[1280,128]{1,0:T(8,128)(2,1)}, bf16[1280,128]{1,0:T(8,128)(2,1)S(1)}, u32[]{:S(2)}) copy-start(bf16[1280,128]{1,0:T(8,128)(2,1)S(1)} %collective-permute-done.2) | copy-start | bytes 983044
  120.8 4.1 %collective-permute-start.6 = (bf16[1024,256]{1,0:T(8,128)(2,1)}, bf16[1024,256]{1,0:T(8,128)(2,1)S(1)}, u32[]{:S(2)}, u32[]{:S(2)}) collective-permute-start(bf16[1024,256]{1,0:T(8,128)(2,1)} %collective-permute-done.3), channel_id=1, source_target_pairs={{0,1},{1,0},{2,3},{3,2},{4,5},{5,4},{6,7},{7,6},{8,9},{9,8},{10,11... | collective-permute-start | bytes 1572872 | tf_op jit(solution)/shard_map/ppermute | solution.py:17
  124.9 1.1 copy-start.11
  126.0 11.2 %collective-permute-start.7 = (bf16[1024,256]{1,0:T(8,128)(2,1)}, bf16[1024,256]{1,0:T(8,128)(2,1)}, u32[]{:S(2)}, u32[]{:S(2)}) collective-permute-start(bf16[1024,256]{1,0:T(8,128)(2,1)} %add_convert_fusion), channel_id=1, source_target_pairs={{0,1},{1,0},{2,3},{3,2},{4,5},{5,4},{6,7},{7,6},{8,9},{9,8},{10,11... | collective-permute-start | bytes 1572872 | tf_op jit(solution)/shard_map/ppermute | solution.py:17
  128.7 5.7 %copy-start.17 = (s32[32]{0:T(128)S(1)}, s32[32]{0:T(128)}, u32[]{:S(2)}) copy-start(s32[32]{0:T(128)} %param.8) | copy-start | bytes 388
  128.7 5.8 %copy-start.5 = (bf16[1280,128]{1,0:T(8,128)(2,1)S(1)}, bf16[1280,128]{1,0:T(8,128)(2,1)}, u32[]{:S(2)}) copy-start(bf16[1280,128]{1,0:T(8,128)(2,1)} %copy-done.4) | copy-start | bytes 983044
  129.9 5.3 %copy-start.12 = (bf16[1024,256]{1,0:T(8,128)(2,1)S(1)}, bf16[1024,256]{1,0:T(8,128)(2,1)}, u32[]{:S(2)}) copy-start(bf16[1024,256]{1,0:T(8,128)(2,1)} %copy-done.11) | copy-start | bytes 1572868
  129.9 22.1 %all-to-all-start.1 = ((bf16[4,1280,128]{1,2,0:T(8,128)(2,1)}), bf16[4,1280,128]{1,2,0:T(8,128)(2,1)S(1)}, u32[]{:S(2)}, u32[]{:S(2)}) async-start(bf16[4,1280,128]{1,2,0:T(8,128)(2,1)} %broadcast_in_dim.13), calls=%async_computation.1 | async-start | bytes 2621440 | tf_op jit(solution)/shard_map/all_to_all | solution.py:56
  152.0 2.4 copy-start.3
  156.0 8.9 %copy-start.14 = (bf16[256,256]{1,0:T(8,128)(2,1)S(1)}, bf16[256,256]{1,0:T(8,128)(2,1)}, u32[]{:S(2)}) copy-start(bf16[256,256]{1,0:T(8,128)(2,1)} %fusion.35) | copy-start | bytes 393220
  156.0 8.9 %copy-start.15 = (bf16[256,256]{1,0:T(8,128)(2,1)S(1)}, bf16[256,256]{1,0:T(8,128)(2,1)}, u32[]{:S(2)}) copy-start(bf16[256,256]{1,0:T(8,128)(2,1)} %fusion.36) | copy-start | bytes 393220
  156.0 8.9 %copy-start.16 = (bf16[1,256,256]{2,1,0:T(8,128)(2,1)S(1)}, bf16[1,256,256]{2,1,0:T(8,128)(2,1)}, u32[]{:S(2)}) copy-start(bf16[1,256,256]{2,1,0:T(8,128)(2,1)} %convolution_bitcast_fusion) | copy-start | bytes 393220
  156.0 18.5 %collective-permute-start.14 = (bf16[1024,128]{1,0:T(8,128)(2,1)}, bf16[1024,128]{1,0:T(8,128)(2,1)}, u32[]{:S(2)}, u32[]{:S(2)}) collective-permute-start(bf16[1024,128]{1,0:T(8,128)(2,1)} %slice.89), channel_id=1, source_target_pairs={{0,1},{1,0},{2,3},{3,2},{4,5},{5,4},{6,7},{7,6},{8,9},{9,8},{10,11... | collective-permute-start | bytes 786440 | tf_op jit(solution)/shard_map/ppermute | solution.py:17
  165.9 4.1 %slice-start = ((bf16[4,1280,128]{1,2,0:T(8,128)(2,1)}), bf16[4,256,128]{1,2,0:T(8,128)(2,1)S(1)}, s32[]{:S(2)}) async-start(bf16[4,1280,128]{1,2,0:T(8,128)(2,1)} %copy-done.3), calls=%async_computation.5 | async-start | bytes 524288 | tf_op jit(solution)/shard_map/slice | solution.py:134
  165.9 52.6 %all-to-all-start.2 = ((bf16[4,512,512]{2,1,0:T(8,128)(2,1)}), bf16[4,512,512]{2,1,0:T(8,128)(2,1)S(1)}, u32[]{:S(2)}, u32[]{:S(2)}) async-start(bf16[4,512,512]{2,1,0:T(8,128)(2,1)} %pad_maximum_fusion), calls=%async_computation.2 | async-start | bytes 4194304 | tf_op jit(solution)/shard_map/all_to_all | solution.py:56
  170.8 3.5 %slice-start.1 = ((bf16[512,128]{1,0:T(8,128)(2,1)}), bf16[384,128]{1,0:T(8,128)(2,1)S(1)}, s32[]{:S(2)}) async-start(bf16[512,128]{1,0:T(8,128)(2,1)} %fusion.37), calls=%async_computation.6 | async-start | bytes 196608 | tf_op jit(solution)/shard_map/slice | solution.py:115
  170.8 3.5 %copy-start.2 = (bf16[2,2,256,256]{3,2,1,0:T(8,128)(2,1)S(1)}, bf16[2,2,256,256]{3,2,1,0:T(8,128)(2,1)}, u32[]{:S(2)}) copy-start(bf16[2,2,256,256]{3,2,1,0:T(8,128)(2,1)} %reverse_select_fusion.1) | copy-start | bytes 1572868
  172.0 3.7 %slice-start.2 = ((bf16[512,128]{1,0:T(8,128)(2,1)}), bf16[384,128]{1,0:T(8,128)(2,1)S(1)}, s32[]{:S(2)}) async-start(bf16[512,128]{1,0:T(8,128)(2,1)} %fusion.38), calls=%async_computation.7 | async-start | bytes 196608 | tf_op jit(solution)/shard_map/slice | solution.py:115
  172.1 3.8 %collective-permute-start.8 = (bf16[16,128,128]{2,1,0:T(8,128)(2,1)S(1)}, bf16[16,128,128]{2,1,0:T(8,128)(2,1)S(1)}, u32[]{:S(2)}, u32[]{:S(2)}) collective-permute-start(bf16[16,128,128]{2,1,0:T(8,128)(2,1)S(1)} %get-tuple-element.46), channel_id=1, source_target_pairs={{0,1},{1,0},{2,3},{3,2},{4,5},{5,4},{6,7},{7,6},{8,9},{9,8},{10,11... | collective-permute-start | bytes 1572872 | tf_op jit(solution)/shard_map/ppermute | solution.py:17
  183.8 19.1 %collective-permute-start.11 = (bf16[8,128,128]{1,2,0:T(8,128)(2,1)}, bf16[8,128,128]{1,2,0:T(8,128)(2,1)}, u32[]{:S(2)}, u32[]{:S(2)}) collective-permute-start(bf16[8,128,128]{1,2,0:T(8,128)(2,1)} %bitcast.121), channel_id=1, source_target_pairs={{0,384},{128,0},{256,128},{384,256},{1,385},{129,1},{257,129},{385... | collective-permute-start | bytes 786440 | tf_op jit(solution)/shard_map/ppermute | solution.py:13
  190.4 15.8 %collective-permute-start.10 = (bf16[8,128,128]{1,2,0:T(8,128)(2,1)}, bf16[8,128,128]{1,2,0:T(8,128)(2,1)}, u32[]{:S(2)}, u32[]{:S(2)}) collective-permute-start(bf16[8,128,128]{1,2,0:T(8,128)(2,1)} %bitcast.119), channel_id=1, source_target_pairs={{0,256},{128,384},{256,0},{384,128},{1,257},{129,385},{257,1},{385... | collective-permute-start | bytes 786440 | tf_op jit(solution)/shard_map/ppermute | solution.py:13
  194.7 13.3 %collective-permute-start.9 = (bf16[8,128,128]{1,2,0:T(8,128)(2,1)}, bf16[8,128,128]{1,2,0:T(8,128)(2,1)}, u32[]{:S(2)}, u32[]{:S(2)}) collective-permute-start(bf16[8,128,128]{1,2,0:T(8,128)(2,1)} %bitcast.120), channel_id=1, source_target_pairs={{0,128},{128,256},{256,384},{384,0},{1,129},{129,257},{257,385},{3... | collective-permute-start | bytes 786440 | tf_op jit(solution)/shard_map/ppermute | solution.py:13
  198.1 15.3 %collective-permute-start.17 = (bf16[256,384]{1,0:T(8,128)(2,1)}, bf16[256,384]{1,0:T(8,128)(2,1)}, u32[]{:S(2)}, u32[]{:S(2)}) collective-permute-start(bf16[256,384]{1,0:T(8,128)(2,1)} %get-tuple-element.49), channel_id=1, source_target_pairs={{0,96},{32,0},{64,32},{96,64},{1,97},{33,1},{65,33},{97,65},{2,98}... | collective-permute-start | bytes 589832 | tf_op jit(solution)/shard_map/ppermute | solution.py:13
  200.0 17.2 %collective-permute-start.16 = (bf16[256,384]{1,0:T(8,128)(2,1)}, bf16[256,384]{1,0:T(8,128)(2,1)}, u32[]{:S(2)}, u32[]{:S(2)}) collective-permute-start(bf16[256,384]{1,0:T(8,128)(2,1)} %get-tuple-element.48), channel_id=1, source_target_pairs={{0,64},{32,96},{64,0},{96,32},{1,65},{33,97},{65,1},{97,33},{2,66}... | collective-permute-start | bytes 589832 | tf_op jit(solution)/shard_map/ppermute | solution.py:13
  202.8 14.4 %collective-permute-start.15 = (bf16[256,384]{1,0:T(8,128)(2,1)}, bf16[256,384]{1,0:T(8,128)(2,1)S(1)}, u32[]{:S(2)}, u32[]{:S(2)}) collective-permute-start(bf16[256,384]{1,0:T(8,128)(2,1)} %get-tuple-element.47), channel_id=1, source_target_pairs={{0,32},{32,64},{64,96},{96,0},{1,33},{33,65},{65,97},{97,1},{2,34}... | collective-permute-start | bytes 589832 | tf_op jit(solution)/shard_map/ppermute | solution.py:13
  209.5 7.8 %copy-start.6 = (bf16[8,128,128]{1,2,0:T(8,128)(2,1)}, bf16[8,128,128]{1,2,0:T(8,128)(2,1)S(1)}, u32[]{:S(2)}) copy-start(bf16[8,128,128]{1,2,0:T(8,128)(2,1)S(1)} %get-tuple-element.37) | copy-start | bytes 786436
  209.5 7.8 %copy-start.8 = (bf16[8,128,128]{1,2,0:T(8,128)(2,1)}, bf16[8,128,128]{1,2,0:T(8,128)(2,1)S(1)}, u32[]{:S(2)}) copy-start(bf16[8,128,128]{1,2,0:T(8,128)(2,1)S(1)} %get-tuple-element.38) | copy-start | bytes 786436
  209.5 7.8 %copy-start.9 = (bf16[8,128,128]{1,2,0:T(8,128)(2,1)}, bf16[8,128,128]{1,2,0:T(8,128)(2,1)S(1)}, u32[]{:S(2)}) copy-start(bf16[8,128,128]{1,2,0:T(8,128)(2,1)S(1)} %get-tuple-element.39) | copy-start | bytes 786436
  209.5 7.8 %copy-start.10 = (bf16[8,128,128]{1,2,0:T(8,128)(2,1)}, bf16[8,128,128]{1,2,0:T(8,128)(2,1)S(1)}, u32[]{:S(2)}) copy-start(bf16[8,128,128]{1,2,0:T(8,128)(2,1)S(1)} %get-tuple-element.40) | copy-start | bytes 786436
  210.8 24.0 %collective-permute-start.12 = (bf16[8,512,128]{1,2,0:T(8,128)(2,1)}, bf16[8,512,128]{1,2,0:T(8,128)(2,1)}, u32[]{:S(2)}, u32[]{:S(2)}) collective-permute-start(bf16[8,512,128]{1,2,0:T(8,128)(2,1)} %pad_maximum_fusion.5), channel_id=1, source_target_pairs={{0,1},{1,0},{2,3},{3,2},{4,5},{5,4},{6,7},{7,6},{8,9},{9,8},{10,11... | collective-permute-start | bytes 3145736 | tf_op jit(solution)/shard_map/ppermute | solution.py:17
  219.4 13.6 %all-to-all-start.3 = ((bf16[4,256,384]{2,1,0:T(8,128)(2,1)}), bf16[4,256,384]{2,1,0:T(8,128)(2,1)S(1)}, u32[]{:S(2)}, u32[]{:S(2)}) async-start(bf16[4,256,384]{2,1,0:T(8,128)(2,1)} %broadcast_in_dim.15), calls=%async_computation.3 | async-start | bytes 1572864 | tf_op jit(solution)/shard_map/all_to_all | solution.py:56
  222.9 10.3 %copy-start.7 = (bf16[8,128,128]{1,2,0:T(8,128)(2,1)S(1)}, bf16[8,128,128]{1,2,0:T(8,128)(2,1)}, u32[]{:S(2)}) copy-start(bf16[8,128,128]{1,2,0:T(8,128)(2,1)} %copy-done.6) | copy-start | bytes 786436
  225.1 9.7 %collective-permute-start.13 = (bf16[512,256]{1,0:T(8,128)(2,1)S(1)}, bf16[512,256]{1,0:T(8,128)(2,1)S(1)}, u32[]{:S(2)}, u32[]{:S(2)}) collective-permute-start(bf16[512,256]{1,0:T(8,128)(2,1)S(1)} %slice.111), channel_id=1, source_target_pairs={{0,1},{1,0},{2,3},{3,2},{4,5},{5,4},{6,7},{7,6},{8,9},{9,8},{10,11... | collective-permute-start | bytes 786440 | tf_op jit(solution)/shard_map/ppermute | solution.py:17

commit v4 on v3

--- a/solution.py
+++ b/solution.py
@@ -132,8 +132,9 @@
     held = panel.shape[0]
     side = early[..., 3 * own_width :]
     side = jnp.concatenate([side[:, : 2 * held], third[:, tokens:], side[:, 3 * held :]], 1)
-    ordered = block_panels(side, panel_slot, h, k)
+    ordered = block_panels(after(side, factors), panel_slot, h, k)
     rows_got = [pick(ordered, x)] + [shifted(pick(ordered, (x + s) % 4), "x", s) for s in SHIFTS]
+    got, quarter = together(got, quarter)
     rows_got = jnp.stack(rows_got)
     left = jnp.concatenate([pick(rows_got, (x - (h ^ m)) % 4) for m in (0, 1, 3, 2)], 1)
     left_other = swapped(left, "k", 1)

time: 278 us -> 287 us (1.032)
  waiting for transfers between devices: 76.9 us -> 93.4 us
  starting transfers between devices: 94.3 us -> 88.4 us
    ppermute x6, waiting for transfers between devices: 5.68 us -> 16.7 us  [shifted(): lax.ppermute(value, axis, [(i, (i + shift) % size) for i in range(size)])]
    ppermute x12, starting transfers between devices: 60.1 us -> 50.5 us  [swapped(): lax.ppermute(value, axis, [(i, i ^ mask) for i in range(lax.axis_size(axi...]
    ppermute x12, waiting for transfers between devices: 57.2 us -> 63.4 us  [swapped(): lax.ppermute(value, axis, [(i, i ^ mask) for i in range(lax.axis_size(axi...]
    ppermute x6, starting transfers between devices: 17 us -> 20.2 us  [shifted(): lax.ppermute(value, axis, [(i, (i + shift) % size) for i in range(size)])]
  transfers between devices with their start and end apart: 22 -> 22, of which waited for: 9 -> 11; matrix products, arithmetic and copies ran while one was open for 18% -> 17% of each run, Pallas kernels for 0% -> 0%
where the time goes in v4:
time: 287 us; the launch traced here: 285 us
  waiting for transfers between devices  93.4 us (33%)
  starting transfers between devices  88.4 us (31%)
  blocking collectives  36 us (13%)
  matrix products  27.1 us (9%)
  local copies, waits for them, and re-layouts  24 us (8%)
  other arithmetic  15 us (5%)
    ppermute x12, waiting for transfers between devices, swapped(): lax.ppermute(value, axis, [(i, i ^ mask) for i in range(lax.axis_size(axi...  63.4 us
    ppermute x12, starting transfers between devices, swapped(): lax.ppermute(value, axis, [(i, i ^ mask) for i in range(lax.axis_size(axi...  50.5 us
    all_to_all x1, blocking collectives, exchanged(): return lax.all_to_all(pieces, axes, 0, 0, tiled=True)  36 us
    ppermute x6, starting transfers between devices, shifted(): lax.ppermute(value, axis, [(i, (i + shift) % size) for i in range(size)])  20.2 us
    all_to_all x4, starting transfers between devices, exchanged(): return lax.all_to_all(pieces, axes, 0, 0, tiled=True)  17.7 us
    ppermute x6, waiting for transfers between devices, shifted(): lax.ppermute(value, axis, [(i, (i + shift) % size) for i in range(size)])  16.7 us
    all_to_all x4, waiting for transfers between devices, exchanged(): return lax.all_to_all(pieces, axes, 0, 0, tiled=True)  13.2 us
    dot_general x8, matrix products, contract_rows(): lax.dot_general(first_operand, second_operand, (((0,), (0,)), ((), ())),...  12.6 us
  transfers between devices with their start and end apart: 22, of which 11 were waited for; matrix products, arithmetic and copies ran while one was open for 17% of the time, Pallas kernels for 0%

profile of v4, /device:TPU:1, one launch (start us, length us, event | category | flops | bytes accessed | tf_op | source)
XLA Modules:
  0.0 285.5 jit_solution(13466001327602727178)
XLA Ops:
  2.6 13.3 %collective-permute-start.1 = (bf16[1280,128]{1,0:T(8,128)(2,1)S(1)}, bf16[1280,128]{1,0:T(8,128)(2,1)S(1)}, u32[]{:S(2)}, u32[]{:S(2)}) collective-permute-start(bf16[1280,128]{1,0:T(8,128)(2,1)S(1)} %pad_maximum_fusion.8), channel_id=1, source_target_pairs={{0,6},{2,4},{4,2},{6,0},{1,7},{3,5},{5,3},{7,1},{8,14},{10,12},{12... | collective-permute-start | bytes 983048 | tf_op jit(solution)/shard_map/ppermute | solution.py:17
  15.9 5.2 %collective-permute-start = (bf16[1280,128]{1,0:T(8,128)(2,1)S(1)}, bf16[1280,128]{1,0:T(8,128)(2,1)}, u32[]{:S(2)}, u32[]{:S(2)}) collective-permute-start(bf16[1280,128]{1,0:T(8,128)(2,1)S(1)} %pad_maximum_fusion.8), channel_id=1, source_target_pairs={{0,2},{2,0},{4,6},{6,4},{1,3},{3,1},{5,7},{7,5},{8,10},{10,8},{12,... | collective-permute-start | bytes 983048 | tf_op jit(solution)/shard_map/ppermute | solution.py:17
  21.0 22.9 %collective-permute-done.1 = bf16[1280,128]{1,0:T(8,128)(2,1)S(1)} collective-permute-done((bf16[1280,128]{1,0:T(8,128)(2,1)S(1)}, bf16[1280,128]{1,0:T(8,128)(2,1)S(1)}, u32[]{:S(2)}, u32[]{:S(2)}) %collective-permute-start.1) | collective-permute-done | bytes 327712 | tf_op jit(solution)/shard_map/ppermute | solution.py:17
  43.9 3.9 %collective-permute-done = bf16[1280,128]{1,0:T(8,128)(2,1)} collective-permute-done((bf16[1280,128]{1,0:T(8,128)(2,1)S(1)}, bf16[1280,128]{1,0:T(8,128)(2,1)}, u32[]{:S(2)}, u32[]{:S(2)}) %collective-permute-start) | collective-permute-done | bytes 327712 | tf_op jit(solution)/shard_map/ppermute | solution.py:17
  49.8 2.4 broadcast_in_dim.12
  52.2 5.0 %all-to-all-start = ((bf16[4,1024,512]{2,1,0:T(8,128)(2,1)}), bf16[4,1024,512]{2,1,0:T(8,128)(2,1)}, u32[]{:S(2)}, u32[]{:S(2)}) async-start(bf16[4,1024,512]{2,1,0:T(8,128)(2,1)} %broadcast_in_dim.12), calls=%async_computation | async-start | bytes 8388608 | tf_op jit(solution)/shard_map/all_to_all | solution.py:56
  57.3 2.9 %collective-permute-start.4 = (bf16[1024,256]{1,0:T(8,128)(2,1)}, bf16[1024,256]{1,0:T(8,128)(2,1)S(1)}, u32[]{:S(2)}, u32[]{:S(2)}) collective-permute-start(bf16[1024,256]{1,0:T(8,128)(2,1)} %param.6), channel_id=1, source_target_pairs={{0,1},{1,0},{2,3},{3,2},{4,5},{5,4},{6,7},{7,6},{8,9},{9,8},{10,11... | collective-permute-start | bytes 1572872 | tf_op jit(solution)/shard_map/ppermute | solution.py:17
  60.4 4.1 %collective-permute-start.2 = (bf16[1280,128]{1,0:T(8,128)(2,1)}, bf16[1280,128]{1,0:T(8,128)(2,1)S(1)}, u32[]{:S(2)}, u32[]{:S(2)}) collective-permute-start(bf16[1280,128]{1,0:T(8,128)(2,1)} %collective-permute-done), channel_id=1, source_target_pairs={{0,6},{2,4},{4,2},{6,0},{1,7},{3,5},{5,3},{7,1},{8,14},{10,12},{12... | collective-permute-start | bytes 983048 | tf_op jit(solution)/shard_map/ppermute | solution.py:17
  64.5 6.2 %collective-permute-start.3 = (bf16[1024,256]{1,0:T(8,128)(2,1)}, bf16[1024,256]{1,0:T(8,128)(2,1)}, u32[]{:S(2)}, u32[]{:S(2)}) collective-permute-start(bf16[1024,256]{1,0:T(8,128)(2,1)} %param.6), channel_id=1, source_target_pairs={{0,2},{2,0},{4,6},{6,4},{1,3},{3,1},{5,7},{7,5},{8,10},{10,8},{12,... | collective-permute-start | bytes 1572872 | tf_op jit(solution)/shard_map/ppermute | solution.py:17
  70.7 2.5 collective-permute-start.5
  74.3 2.2 fusion.35
  76.9 1.3 convolution_add_fusion
  78.2 2.0 fusion.36
  81.4 11.7 %collective-permute-done.2 = bf16[1280,128]{1,0:T(8,128)(2,1)S(1)} collective-permute-done((bf16[1280,128]{1,0:T(8,128)(2,1)}, bf16[1280,128]{1,0:T(8,128)(2,1)S(1)}, u32[]{:S(2)}, u32[]{:S(2)}) %collective-permute-start.2) | collective-permute-done | bytes 327712 | tf_op jit(solution)/shard_map/ppermute | solution.py:17
  93.1 24.6 %collective-permute-done.3 = bf16[1024,256]{1,0:T(8,128)(2,1)} collective-permute-done((bf16[1024,256]{1,0:T(8,128)(2,1)}, bf16[1024,256]{1,0:T(8,128)(2,1)}, u32[]{:S(2)}, u32[]{:S(2)}) %collective-permute-start.3) | collective-permute-done | bytes 524320 | tf_op jit(solution)/shard_map/ppermute | solution.py:17
  117.7 3.0 %collective-permute-start.6 = (bf16[1024,256]{1,0:T(8,128)(2,1)}, bf16[1024,256]{1,0:T(8,128)(2,1)S(1)}, u32[]{:S(2)}, u32[]{:S(2)}) collective-permute-start(bf16[1024,256]{1,0:T(8,128)(2,1)} %collective-permute-done.3), channel_id=1, source_target_pairs={{0,1},{1,0},{2,3},{3,2},{4,5},{5,4},{6,7},{7,6},{8,9},{9,8},{10,11... | collective-permute-start | bytes 1572872 | tf_op jit(solution)/shard_map/ppermute | solution.py:17
  120.7 1.3 fusion.26
  123.5 2.3 collective-permute-start.7
  127.4 4.6 %all-to-all-start.1 = ((bf16[4,1280,128]{1,2,0:T(8,128)(2,1)}), bf16[4,1280,128]{1,2,0:T(8,128)(2,1)S(1)}, u32[]{:S(2)}, u32[]{:S(2)}) async-start(bf16[4,1280,128]{1,2,0:T(8,128)(2,1)} %broadcast_in_dim.13), calls=%async_computation.1 | async-start | bytes 2621440 | tf_op jit(solution)/shard_map/all_to_all | solution.py:56
  132.7 2.0 convolution_bitcast_fusion
  134.8 4.8 %fusion.3 = bf16[4,512,512]{2,1,0:T(8,128)(2,1)S(1)} fusion(bf16[4,1024,512]{2,1,0:T(8,128)(2,1)} %all-to-all-done, bf16[1024,256]{1,0:T(8,128)(2,1)} %collective-permute-done.7, bf16[1024,256]{1,0:T(8,128)(2,1)} %add_convert_fusion), kind=kOutput, calls=%fused_computation.37 | convolution fusion | flops 2149580800 | bytes 7340032 | tf_op jit(solution)/shard_map/btf,tc->bfc/dot_general | solution.py:31
  139.7 9.8 %all-to-all-done.1 = bf16[4,1280,128]{1,2,0:T(8,128)(2,1)S(1)} async-done(((bf16[4,1280,128]{1,2,0:T(8,128)(2,1)}), bf16[4,1280,128]{1,2,0:T(8,128)(2,1)S(1)}, u32[]{:S(2)}, u32[]{:S(2)}) %all-to-all-start.1) | async-done | bytes 1310752 | tf_op jit(solution)/shard_map/all_to_all | solution.py:56
  149.5 2.4 convolution_convert_fusion
  151.9 1.5 pad_maximum_fusion
  156.8 3.2 %collective-permute-start.8 = (bf16[1024,128]{1,0:T(8,128)(2,1)}, bf16[1024,128]{1,0:T(8,128)(2,1)}, u32[]{:S(2)}, u32[]{:S(2)}) collective-permute-start(bf16[1024,128]{1,0:T(8,128)(2,1)} %slice.89), channel_id=1, source_target_pairs={{0,1},{1,0},{2,3},{3,2},{4,5},{5,4},{6,7},{7,6},{8,9},{9,8},{10,11... | collective-permute-start | bytes 786440 | tf_op jit(solution)/shard_map/ppermute | solution.py:17
  160.9 4.0 %all-to-all-start.2 = ((bf16[4,512,512]{2,1,0:T(8,128)(2,1)}), bf16[4,512,512]{2,1,0:T(8,128)(2,1)S(1)}, u32[]{:S(2)}, u32[]{:S(2)}) async-start(bf16[4,512,512]{2,1,0:T(8,128)(2,1)} %pad_maximum_fusion), calls=%async_computation.2 | async-start | bytes 4194304 | tf_op jit(solution)/shard_map/all_to_all | solution.py:56
  164.9 1.6 convolution_bitcast_fusion.1
  167.9 2.2 collective-permute-start.9
  173.3 2.9 %gather_fusion = bf16[32,128,128]{2,1,0:T(8,128)(2,1)} fusion(bf16[32,128,128]{2,1,0:T(8,128)(2,1)} %pad_maximum_fusion.5, s32[1024]{0:T(1024)S(1)} %pad_clamp_fusion), kind=kCustom, calls=%fused_computation | custom fusion | bytes 2097280 | tf_op jit(solution)/shard_map/jit(_take)/gather | solution.py:70
  176.2 2.1 constant_dynamic-slice_fusion.3
  178.3 1.8 copy.38
  180.1 1.8 copy.37
  182.7 3.6 %collective-permute-start.10 = (bf16[8,128,128]{1,2,0:T(8,128)(2,1)}, bf16[8,128,128]{1,2,0:T(8,128)(2,1)}, u32[]{:S(2)}, u32[]{:S(2)}) collective-permute-start(bf16[8,128,128]{1,2,0:T(8,128)(2,1)} %bitcast.121), channel_id=1, source_target_pairs={{0,128},{128,256},{256,384},{384,0},{1,129},{129,257},{257,385},{3... | collective-permute-start | bytes 786440 | tf_op jit(solution)/shard_map/ppermute | solution.py:13
  186.4 4.3 %collective-permute-start.11 = (bf16[8,128,128]{1,2,0:T(8,128)(2,1)}, bf16[8,128,128]{1,2,0:T(8,128)(2,1)}, u32[]{:S(2)}, u32[]{:S(2)}) collective-permute-start(bf16[8,128,128]{1,2,0:T(8,128)(2,1)} %bitcast.120), channel_id=1, source_target_pairs={{0,256},{128,384},{256,0},{384,128},{1,257},{129,385},{257,1},{385... | collective-permute-start | bytes 786440 | tf_op jit(solution)/shard_map/ppermute | solution.py:13
  190.7 3.1 %collective-permute-start.12 = (bf16[8,128,128]{1,2,0:T(8,128)(2,1)}, bf16[8,128,128]{1,2,0:T(8,128)(2,1)}, u32[]{:S(2)}, u32[]{:S(2)}) collective-permute-start(bf16[8,128,128]{1,2,0:T(8,128)(2,1)} %bitcast.119), channel_id=1, source_target_pairs={{0,384},{128,0},{256,128},{384,256},{1,385},{129,1},{257,129},{385... | collective-permute-start | bytes 786440 | tf_op jit(solution)/shard_map/ppermute | solution.py:13
  195.8 2.3 collective-permute-done.10
  198.1 4.3 %collective-permute-done.11 = bf16[8,128,128]{1,2,0:T(8,128)(2,1)} collective-permute-done((bf16[8,128,128]{1,2,0:T(8,128)(2,1)}, bf16[8,128,128]{1,2,0:T(8,128)(2,1)}, u32[]{:S(2)}, u32[]{:S(2)}) %collective-permute-start.11) | collective-permute-done | bytes 262176 | tf_op jit(solution)/shard_map/ppermute | solution.py:13
  205.1 3.0 %collective-permute-start.16 = (bf16[8,512,128]{1,2,0:T(8,128)(2,1)}, bf16[8,512,128]{1,2,0:T(8,128)(2,1)}, u32[]{:S(2)}, u32[]{:S(2)}) collective-permute-start(bf16[8,512,128]{1,2,0:T(8,128)(2,1)} %pad_maximum_fusion.7), channel_id=1, source_target_pairs={{0,1},{1,0},{2,3},{3,2},{4,5},{5,4},{6,7},{7,6},{8,9},{9,8},{10,11... | collective-permute-start | bytes 3145736 | tf_op jit(solution)/shard_map/ppermute | solution.py:17
  209.1 1.9 collective-permute-start.13
  211.0 1.9 collective-permute-start.14
  212.9 5.3 %collective-permute-start.15 = (bf16[256,384]{1,0:T(8,128)(2,1)S(1)}, bf16[256,384]{1,0:T(8,128)(2,1)}, u32[]{:S(2)}, u32[]{:S(2)}) collective-permute-start(bf16[256,384]{1,0:T(8,128)(2,1)S(1)} %get-tuple-element.55), channel_id=1, source_target_pairs={{0,96},{32,0},{64,32},{96,64},{1,97},{33,1},{65,33},{97,65},{2,98}... | collective-permute-start | bytes 589832 | tf_op jit(solution)/shard_map/ppermute | solution.py:13
  219.6 8.8 %collective-permute-done.14 = bf16[256,384]{1,0:T(8,128)(2,1)} collective-permute-done((bf16[256,384]{1,0:T(8,128)(2,1)}, bf16[256,384]{1,0:T(8,128)(2,1)}, u32[]{:S(2)}, u32[]{:S(2)}) %collective-permute-start.14) | collective-permute-done | bytes 196640 | tf_op jit(solution)/shard_map/ppermute | solution.py:13
  230.5 4.1 %all-to-all-start.3 = ((bf16[4,256,384]{2,1,0:T(8,128)(2,1)}), bf16[4,256,384]{2,1,0:T(8,128)(2,1)S(1)}, u32[]{:S(2)}, u32[]{:S(2)}) async-start(bf16[4,256,384]{2,1,0:T(8,128)(2,1)} %broadcast_in_dim.15), calls=%async_computation.3 | async-start | bytes 1572864 | tf_op jit(solution)/shard_map/all_to_all | solution.py:56
  236.8 2.7 collective-permute-start.17
  239.5 1.6 fusion.10
  241.1 1.7 fusion
  242.8 3.4 %all-to-all-done.3 = bf16[4,256,384]{2,1,0:T(8,128)(2,1)S(1)} async-done(((bf16[4,256,384]{2,1,0:T(8,128)(2,1)}), bf16[4,256,384]{2,1,0:T(8,128)(2,1)S(1)}, u32[]{:S(2)}, u32[]{:S(2)}) %all-to-all-start.3) | async-done | bytes 786464 | tf_op jit(solution)/shard_map/all_to_all | solution.py:56
  246.6 36.0 %all_to_all.25 = bf16[4,256,640]{2,1,0:T(8,128)(2,1)S(1)} all-to-all(bf16[4,256,640]{2,1,0:T(8,128)(2,1)S(1)} %pad_maximum_fusion.2), channel_id=1, replica_groups=mesh['x'=4,'l'=4,'y'=4,'h'=4,'k'=2] {'l'}, dimensions={0} | all-to-all | bytes 2621440 | tf_op jit(solution)/shard_map/all_to_all | solution.py:56
  (106 shorter events, 34.3 us)
Async XLA Ops:
  0.6 1.0 copy-start
  0.6 49.0 %copy-start.1 = (bf16[1024,128]{1,0:T(8,128)(2,1)S(1)}, bf16[1024,128]{1,0:T(8,128)(2,1)}, u32[]{:S(2)}) copy-start(bf16[1024,128]{1,0:T(8,128)(2,1)} %param.5) | copy-start | bytes 786436
  2.6 41.3 %collective-permute-start.1 = (bf16[1280,128]{1,0:T(8,128)(2,1)S(1)}, bf16[1280,128]{1,0:T(8,128)(2,1)S(1)}, u32[]{:S(2)}, u32[]{:S(2)}) collective-permute-start(bf16[1280,128]{1,0:T(8,128)(2,1)S(1)} %pad_maximum_fusion.8), channel_id=1, source_target_pairs={{0,6},{2,4},{4,2},{6,0},{1,7},{3,5},{5,3},{7,1},{8,14},{10,12},{12... | collective-permute-start | bytes 983048 | tf_op jit(solution)/shard_map/ppermute | solution.py:17
  15.9 32.0 %collective-permute-start = (bf16[1280,128]{1,0:T(8,128)(2,1)S(1)}, bf16[1280,128]{1,0:T(8,128)(2,1)}, u32[]{:S(2)}, u32[]{:S(2)}) collective-permute-start(bf16[1280,128]{1,0:T(8,128)(2,1)S(1)} %pad_maximum_fusion.8), channel_id=1, source_target_pairs={{0,2},{2,0},{4,6},{6,4},{1,3},{3,1},{5,7},{7,5},{8,10},{10,8},{12,... | collective-permute-start | bytes 983048 | tf_op jit(solution)/shard_map/ppermute | solution.py:17
  52.2 5.1 %copy-start.13 = (bf16[1024,256]{1,0:T(8,128)(2,1)S(1)}, bf16[1024,256]{1,0:T(8,128)(2,1)}, u32[]{:S(2)}) copy-start(bf16[1024,256]{1,0:T(8,128)(2,1)} %param.9) | copy-start | bytes 1572868
  52.2 65.5 %all-to-all-start = ((bf16[4,1024,512]{2,1,0:T(8,128)(2,1)}), bf16[4,1024,512]{2,1,0:T(8,128)(2,1)}, u32[]{:S(2)}, u32[]{:S(2)}) async-start(bf16[4,1024,512]{2,1,0:T(8,128)(2,1)} %broadcast_in_dim.12), calls=%async_computation | async-start | bytes 8388608 | tf_op jit(solution)/shard_map/all_to_all | solution.py:56
  57.3 19.2 %collective-permute-start.4 = (bf16[1024,256]{1,0:T(8,128)(2,1)}, bf16[1024,256]{1,0:T(8,128)(2,1)S(1)}, u32[]{:S(2)}, u32[]{:S(2)}) collective-permute-start(bf16[1024,256]{1,0:T(8,128)(2,1)} %param.6), channel_id=1, source_target_pairs={{0,1},{1,0},{2,3},{3,2},{4,5},{5,4},{6,7},{7,6},{8,9},{9,8},{10,11... | collective-permute-start | bytes 1572872 | tf_op jit(solution)/shard_map/ppermute | solution.py:17
  60.4 32.7 %collective-permute-start.2 = (bf16[1280,128]{1,0:T(8,128)(2,1)}, bf16[1280,128]{1,0:T(8,128)(2,1)S(1)}, u32[]{:S(2)}, u32[]{:S(2)}) collective-permute-start(bf16[1280,128]{1,0:T(8,128)(2,1)} %collective-permute-done), channel_id=1, source_target_pairs={{0,6},{2,4},{4,2},{6,0},{1,7},{3,5},{5,3},{7,1},{8,14},{10,12},{12... | collective-permute-start | bytes 983048 | tf_op jit(solution)/shard_map/ppermute | solution.py:17
  64.5 53.1 %collective-permute-start.3 = (bf16[1024,256]{1,0:T(8,128)(2,1)}, bf16[1024,256]{1,0:T(8,128)(2,1)}, u32[]{:S(2)}, u32[]{:S(2)}) collective-permute-start(bf16[1024,256]{1,0:T(8,128)(2,1)} %param.6), channel_id=1, source_target_pairs={{0,2},{2,0},{4,6},{6,4},{1,3},{3,1},{5,7},{7,5},{8,10},{10,8},{12,... | collective-permute-start | bytes 1572872 | tf_op jit(solution)/shard_map/ppermute | solution.py:17
  70.7 9.5 %collective-permute-start.5 = (bf16[1024,512]{1,0:T(8,128)(2,1)S(1)}, bf16[1024,512]{1,0:T(8,128)(2,1)S(1)}, u32[]{:S(2)}, u32[]{:S(2)}) collective-permute-start(bf16[1024,512]{1,0:T(8,128)(2,1)S(1)} %maximum_maximum_fusion), channel_id=1, source_target_pairs={{0,1},{1,0},{2,3},{3,2},{4,5},{5,4},{6,7},{7,6},{8,9},{9,8},{10,11... | collective-permute-start | bytes 3145736 | tf_op jit(solution)/shard_map/ppermute | solution.py:17
  93.1 32.9 %copy-start.3 = (bf16[1280,128]{1,0:T(8,128)(2,1)}, bf16[1280,128]{1,0:T(8,128)(2,1)S(1)}, u32[]{:S(2)}) copy-start(bf16[1280,128]{1,0:T(8,128)(2,1)S(1)} %collective-permute-done.2) | copy-start | bytes 983044
  117.7 4.7 %collective-permute-start.6 = (bf16[1024,256]{1,0:T(8,128)(2,1)}, bf16[1024,256]{1,0:T(8,128)(2,1)S(1)}, u32[]{:S(2)}, u32[]{:S(2)}) collective-permute-start(bf16[1024,256]{1,0:T(8,128)(2,1)} %collective-permute-done.3), channel_id=1, source_target_pairs={{0,1},{1,0},{2,3},{3,2},{4,5},{5,4},{6,7},{7,6},{8,9},{9,8},{10,11... | collective-permute-start | bytes 1572872 | tf_op jit(solution)/shard_map/ppermute | solution.py:17
  122.4 1.1 copy-start.11
  123.5 11.3 %collective-permute-start.7 = (bf16[1024,256]{1,0:T(8,128)(2,1)}, bf16[1024,256]{1,0:T(8,128)(2,1)}, u32[]{:S(2)}, u32[]{:S(2)}) collective-permute-start(bf16[1024,256]{1,0:T(8,128)(2,1)} %add_convert_fusion), channel_id=1, source_target_pairs={{0,1},{1,0},{2,3},{3,2},{4,5},{5,4},{6,7},{7,6},{8,9},{9,8},{10,11... | collective-permute-start | bytes 1572872 | tf_op jit(solution)/shard_map/ppermute | solution.py:17
  126.2 5.8 %copy-start.14 = (s32[32]{0:T(128)S(1)}, s32[32]{0:T(128)}, u32[]{:S(2)}) copy-start(s32[32]{0:T(128)} %param.8) | copy-start | bytes 388
  126.2 5.8 %copy-start.4 = (bf16[1280,128]{1,0:T(8,128)(2,1)S(1)}, bf16[1280,128]{1,0:T(8,128)(2,1)}, u32[]{:S(2)}) copy-start(bf16[1280,128]{1,0:T(8,128)(2,1)} %copy-done.3) | copy-start | bytes 983044
  127.4 5.4 %copy-start.12 = (bf16[1024,256]{1,0:T(8,128)(2,1)S(1)}, bf16[1024,256]{1,0:T(8,128)(2,1)}, u32[]{:S(2)}) copy-start(bf16[1024,256]{1,0:T(8,128)(2,1)} %copy-done.11) | copy-start | bytes 1572868
  127.4 22.1 %all-to-all-start.1 = ((bf16[4,1280,128]{1,2,0:T(8,128)(2,1)}), bf16[4,1280,128]{1,2,0:T(8,128)(2,1)S(1)}, u32[]{:S(2)}, u32[]{:S(2)}) async-start(bf16[4,1280,128]{1,2,0:T(8,128)(2,1)} %broadcast_in_dim.13), calls=%async_computation.1 | async-start | bytes 2621440 | tf_op jit(solution)/shard_map/all_to_all | solution.py:56
  149.5 2.4 copy-start.2
  153.4 6.6 %slice-start = ((bf16[4,1280,128]{1,2,0:T(8,128)(2,1)}), bf16[4,256,128]{1,2,0:T(8,128)(2,1)S(1)}, s32[]{:S(2)}) async-start(bf16[4,1280,128]{1,2,0:T(8,128)(2,1)} %copy-done.2), calls=%async_computation.5 | async-start | bytes 524288 | tf_op jit(solution)/shard_map/slice | solution.py:134
  156.8 13.4 %collective-permute-start.8 = (bf16[1024,128]{1,0:T(8,128)(2,1)}, bf16[1024,128]{1,0:T(8,128)(2,1)}, u32[]{:S(2)}, u32[]{:S(2)}) collective-permute-start(bf16[1024,128]{1,0:T(8,128)(2,1)} %slice.89), channel_id=1, source_target_pairs={{0,1},{1,0},{2,3},{3,2},{4,5},{5,4},{6,7},{7,6},{8,9},{9,8},{10,11... | collective-permute-start | bytes 786440 | tf_op jit(solution)/shard_map/ppermute | solution.py:17
  160.9 68.7 %all-to-all-start.2 = ((bf16[4,512,512]{2,1,0:T(8,128)(2,1)}), bf16[4,512,512]{2,1,0:T(8,128)(2,1)S(1)}, u32[]{:S(2)}, u32[]{:S(2)}) async-start(bf16[4,512,512]{2,1,0:T(8,128)(2,1)} %pad_maximum_fusion), calls=%async_computation.2 | async-start | bytes 4194304 | tf_op jit(solution)/shard_map/all_to_all | solution.py:56
  164.9 2.8 copy-start.10
  167.7 2.4 slice-start.1
  167.8 3.7 %slice-start.2 = ((bf16[512,128]{1,0:T(8,128)(2,1)}), bf16[384,128]{1,0:T(8,128)(2,1)S(1)}, s32[]{:S(2)}) async-start(bf16[512,128]{1,0:T(8,128)(2,1)} %fusion.38), calls=%async_computation.7 | async-start | bytes 196608 | tf_op jit(solution)/shard_map/slice | solution.py:115
  167.9 4.4 %collective-permute-start.9 = (bf16[16,128,128]{2,1,0:T(8,128)(2,1)S(1)}, bf16[16,128,128]{2,1,0:T(8,128)(2,1)S(1)}, u32[]{:S(2)}, u32[]{:S(2)}) collective-permute-start(bf16[16,128,128]{2,1,0:T(8,128)(2,1)S(1)} %get-tuple-element.52), channel_id=1, source_target_pairs={{0,1},{1,0},{2,3},{3,2},{4,5},{5,4},{6,7},{7,6},{8,9},{9,8},{10,11... | collective-permute-start | bytes 1572872 | tf_op jit(solution)/shard_map/ppermute | solution.py:17
  182.7 15.4 %collective-permute-start.10 = (bf16[8,128,128]{1,2,0:T(8,128)(2,1)}, bf16[8,128,128]{1,2,0:T(8,128)(2,1)}, u32[]{:S(2)}, u32[]{:S(2)}) collective-permute-start(bf16[8,128,128]{1,2,0:T(8,128)(2,1)} %bitcast.121), channel_id=1, source_target_pairs={{0,128},{128,256},{256,384},{384,0},{1,129},{129,257},{257,385},{3... | collective-permute-start | bytes 786440 | tf_op jit(solution)/shard_map/ppermute | solution.py:13
  186.4 16.1 %collective-permute-start.11 = (bf16[8,128,128]{1,2,0:T(8,128)(2,1)}, bf16[8,128,128]{1,2,0:T(8,128)(2,1)}, u32[]{:S(2)}, u32[]{:S(2)}) collective-permute-start(bf16[8,128,128]{1,2,0:T(8,128)(2,1)} %bitcast.120), channel_id=1, source_target_pairs={{0,256},{128,384},{256,0},{384,128},{1,257},{129,385},{257,1},{385... | collective-permute-start | bytes 786440 | tf_op jit(solution)/shard_map/ppermute | solution.py:13
  190.7 11.8 %collective-permute-start.12 = (bf16[8,128,128]{1,2,0:T(8,128)(2,1)}, bf16[8,128,128]{1,2,0:T(8,128)(2,1)}, u32[]{:S(2)}, u32[]{:S(2)}) collective-permute-start(bf16[8,128,128]{1,2,0:T(8,128)(2,1)} %bitcast.119), channel_id=1, source_target_pairs={{0,384},{128,0},{256,128},{384,256},{1,385},{129,1},{257,129},{385... | collective-permute-start | bytes 786440 | tf_op jit(solution)/shard_map/ppermute | solution.py:13
  203.9 5.2 %copy-start.5 = (bf16[8,128,128]{1,2,0:T(8,128)(2,1)}, bf16[8,128,128]{1,2,0:T(8,128)(2,1)S(1)}, u32[]{:S(2)}) copy-start(bf16[8,128,128]{1,2,0:T(8,128)(2,1)S(1)} %get-tuple-element.43) | copy-start | bytes 786436
  203.9 5.2 %copy-start.7 = (bf16[8,128,128]{1,2,0:T(8,128)(2,1)}, bf16[8,128,128]{1,2,0:T(8,128)(2,1)S(1)}, u32[]{:S(2)}) copy-start(bf16[8,128,128]{1,2,0:T(8,128)(2,1)S(1)} %get-tuple-element.44) | copy-start | bytes 786436
  203.9 5.2 %copy-start.8 = (bf16[8,128,128]{1,2,0:T(8,128)(2,1)}, bf16[8,128,128]{1,2,0:T(8,128)(2,1)S(1)}, u32[]{:S(2)}) copy-start(bf16[8,128,128]{1,2,0:T(8,128)(2,1)S(1)} %get-tuple-element.45) | copy-start | bytes 786436
  203.9 5.2 %copy-start.9 = (bf16[8,128,128]{1,2,0:T(8,128)(2,1)}, bf16[8,128,128]{1,2,0:T(8,128)(2,1)S(1)}, u32[]{:S(2)}) copy-start(bf16[8,128,128]{1,2,0:T(8,128)(2,1)S(1)} %get-tuple-element.46) | copy-start | bytes 786436
  205.1 36.0 %collective-permute-start.16 = (bf16[8,512,128]{1,2,0:T(8,128)(2,1)}, bf16[8,512,128]{1,2,0:T(8,128)(2,1)}, u32[]{:S(2)}, u32[]{:S(2)}) collective-permute-start(bf16[8,512,128]{1,2,0:T(8,128)(2,1)} %pad_maximum_fusion.7), channel_id=1, source_target_pairs={{0,1},{1,0},{2,3},{3,2},{4,5},{5,4},{6,7},{7,6},{8,9},{9,8},{10,11... | collective-permute-start | bytes 3145736 | tf_op jit(solution)/shard_map/ppermute | solution.py:17
  209.1 10.5 %collective-permute-start.13 = (bf16[256,384]{1,0:T(8,128)(2,1)}, bf16[256,384]{1,0:T(8,128)(2,1)S(1)}, u32[]{:S(2)}, u32[]{:S(2)}) collective-permute-start(bf16[256,384]{1,0:T(8,128)(2,1)} %get-tuple-element.53), channel_id=1, source_target_pairs={{0,32},{32,64},{64,96},{96,0},{1,33},{33,65},{65,97},{97,1},{2,34}... | collective-permute-start | bytes 589832 | tf_op jit(solution)/shard_map/ppermute | solution.py:13
  211.0 17.4 %collective-permute-start.14 = (bf16[256,384]{1,0:T(8,128)(2,1)}, bf16[256,384]{1,0:T(8,128)(2,1)}, u32[]{:S(2)}, u32[]{:S(2)}) collective-permute-start(bf16[256,384]{1,0:T(8,128)(2,1)} %get-tuple-element.54), channel_id=1, source_target_pairs={{0,64},{32,96},{64,0},{96,32},{1,65},{33,97},{65,1},{97,33},{2,66}... | collective-permute-start | bytes 589832 | tf_op jit(solution)/shard_map/ppermute | solution.py:13
  212.9 15.5 %collective-permute-start.15 = (bf16[256,384]{1,0:T(8,128)(2,1)S(1)}, bf16[256,384]{1,0:T(8,128)(2,1)}, u32[]{:S(2)}, u32[]{:S(2)}) collective-permute-start(bf16[256,384]{1,0:T(8,128)(2,1)S(1)} %get-tuple-element.55), channel_id=1, source_target_pairs={{0,96},{32,0},{64,32},{96,64},{1,97},{33,1},{65,33},{97,65},{2,98}... | collective-permute-start | bytes 589832 | tf_op jit(solution)/shard_map/ppermute | solution.py:13
  230.5 9.0 %copy-start.6 = (bf16[8,128,128]{1,2,0:T(8,128)(2,1)S(1)}, bf16[8,128,128]{1,2,0:T(8,128)(2,1)}, u32[]{:S(2)}) copy-start(bf16[8,128,128]{1,2,0:T(8,128)(2,1)} %copy-done.5) | copy-start | bytes 786436
  230.5 15.7 %all-to-all-start.3 = ((bf16[4,256,384]{2,1,0:T(8,128)(2,1)}), bf16[4,256,384]{2,1,0:T(8,128)(2,1)S(1)}, u32[]{:S(2)}, u32[]{:S(2)}) async-start(bf16[4,256,384]{2,1,0:T(8,128)(2,1)} %broadcast_in_dim.15), calls=%async_computation.3 | async-start | bytes 1572864 | tf_op jit(solution)/shard_map/all_to_all | solution.py:56
  236.8 4.3 %collective-permute-start.17 = (bf16[512,256]{1,0:T(8,128)(2,1)S(1)}, bf16[512,256]{1,0:T(8,128)(2,1)S(1)}, u32[]{:S(2)}, u32[]{:S(2)}) collective-permute-start(bf16[512,256]{1,0:T(8,128)(2,1)S(1)} %slice.115), channel_id=1, source_target_pairs={{0,1},{1,0},{2,3},{3,2},{4,5},{5,4},{6,7},{7,6},{8,9},{9,8},{10,11... | collective-permute-start | bytes 786440 | tf_op jit(solution)/shard_map/ppermute | solution.py:17
